TPU v7x, 256 devices: a whole 4x4x8 slice. The times are simulated.
256 devices in a mesh: tri: 256 (over y, z, x, core).
Axes of the slice: x: 4, y: 4, z: 8, core: 2. Of those that a mesh axis runs over, the one named last changes fastest.
Arguments:
- tiles: float32 [8192, 128, 128], P('tri')
- tile_rows: int32 [8192], P('tri'), may hold values from 0 to 1023, as said below
- tile_cols: int32 [8192], P('tri'), may hold values from 0 to 1023, as said below
- counts: int32 [256], P('tri'), may hold values from 0 to 32, as said below
- block_vectors: float32 [1024, 8, 128], P('tri'), may hold values from -6 to 6
Outputs:
- image: float32 [1024, 8, 128], P('tri')
- gram_mixed: float32 [8, 8], replicated
- gram_image: float32 [8, 8], replicated
Inputs may be any that keep to these rules, and one draw needn't show every extreme that they name: `tile_rows`: the states are cut into 22 segments, segment i spanning tiles i * 1024 // 22 to (i + 1) * 1024 // 22 - 1. Device d below 253 holds block (i, j), i >= j, of the lower triangle taken row by row (d = i * (i + 1) // 2 + j): its slots name row tiles of segment i and column tiles of segment j, no (row tile, column tile) pair twice; the slots of the remaining devices name tile 0. `tile_cols`: the column tile of a slot is at most its row tile. `counts`: devices past the triangle use no slot; the last block uses all 32.
All inputs are finite; a program needn't handle non-finite values.
Results may differ from a plain program's by a relative error of at most 0.0003.
Values sent between devices are 32-bit elements; how exact they have to be, the bound alone decides.
A program may use at most 64 MiB of HBM per device.

v0:
```python
import jax
import jax.numpy as jnp
from jax import lax
from jax.sharding import PartitionSpec as P


def process(carry, tile_list, row_ids, col_ids, row_vectors, col_vectors, limit, group):
    highest = lax.Precision.HIGHEST
    number_groups = (limit + group - 1) // group

    def advance(number, state):
        totals, mixed_gram = state
        first = number * group
        tile_group = lax.dynamic_slice_in_dim(tile_list, first, group, 0)
        row_group = lax.dynamic_slice_in_dim(row_ids, first, group, 0)
        col_group = lax.dynamic_slice_in_dim(col_ids, first, group, 0)
        row_block = lax.dynamic_slice_in_dim(row_vectors, first, group, 0)
        col_block = lax.dynamic_slice_in_dim(col_vectors, first, group, 0)
        live = (first + jnp.arange(group, dtype=jnp.int32) < limit).astype(jnp.float32)[
            :, None, None
        ]
        row_terms = jnp.einsum("kab,kvb->kva", tile_group, col_block, precision=highest) * live
        col_terms = jnp.einsum("kab,kva->kvb", tile_group, row_block, precision=highest) * live
        totals = totals.at[row_group].add(row_terms).at[col_group].add(col_terms)
        return (totals, mixed_gram)

    return lax.fori_loop(0, number_groups, advance, carry)


def per_device(tiles, tile_rows, tile_cols, counts, block_vectors):
    highest = lax.Precision.HIGHEST
    devices = lax.axis_size("tri")
    slots = tile_rows.shape[0]
    group = min(16, slots)
    share = block_vectors.shape[0]
    vectors = block_vectors.shape[1]
    width = block_vectors.shape[2]
    total_tiles = share * devices
    gathered = lax.all_gather(block_vectors, "tri", axis=0, tiled=True)
    col_vectors = gathered[tile_cols]
    row_vectors = gathered[tile_rows]
    carry = (
        jnp.zeros((total_tiles, vectors, width), jnp.float32),
        jnp.zeros((vectors, vectors), jnp.float32),
    )
    totals, mixed_local = process(
        carry, tiles, tile_rows, tile_cols, row_vectors, col_vectors, counts[0], group
    )
    image = lax.psum_scatter(totals, "tri", scatter_dimension=0, tiled=True)
    scale = 1.0 / (total_tiles * width)
    image_local = jnp.einsum("tva,twa->vw", image, image, precision=highest)
    mixed_after = jnp.einsum("tva,twa->vw", block_vectors, image, precision=highest)
    mixed_sum, image_sum = lax.psum((mixed_after, image_local), "tri")
    gram_mixed = mixed_sum * scale
    gram_image = image_sum * scale
    return (image, gram_mixed, gram_image)


def solution(mesh):
    placed = (P("tri", None, None), P("tri"), P("tri"), P("tri"), P("tri", None, None))
    return jax.shard_map(
        per_device,
        mesh=mesh,
        in_specs=placed,
        out_specs=(P("tri", None, None), P(), P()),
        check_vma=False,
    )
```

profile of v0, /device:TPU:1, one launch (start us, length us, event | category | flops | bytes accessed | tf_op | source)
XLA Modules:
  0.0 1507.2 jit_solution(12962307324789088875)
XLA Ops:
  7.2 0.0 copy-start.3
  7.2 0.0 copy-start.2
  7.2 0.0 copy-start
  7.2 0.0 all-gather.2.cloned.1.call-start
  7.2 0.7 all-gather.2.cloned.1.call-update
  7.9 0.0 reduce-scatter.2.cloned.1.call-start
  8.6 0.7 compare_select_fusion.3
  9.3 0.7 compare_select_fusion.2
  10.0 121.0 %all-gather.2.cloned.1.call-done = f32[1024,8,128]{2,1,0:T(8,128)} async-done(((f32[4,8,128]{2,1,0:T(8,128)}), f32[1024,8,128]{2,1,0:T(8,128)}) %all-gather.2.cloned.1.call-update) | async-done | bytes 4194320 | tf_op jit(solution)/shard_map/all_gather | solution.py:39
  131.0 2.8 gather_fusion
  133.8 2.8 gather_fusion.1
  136.5 2.2 broadcast_in_dim.16
  138.7 0.0 copy-done.3
  138.7 0.0 copy-done.2
  138.7 0.0 copy-done
  138.7 7.7 while.10
  138.8 0.7 compare_convert_fusion.2
  139.4 1.7 convolution_multiply_fusion.4
  141.1 0.1 compare_select_fusion.5
  141.2 2.1 scatter_fusion
  143.3 1.0 convolution_multiply_fusion.5
  144.3 2.1 scatter_fusion.1
  146.4 0.0 copy-start.1
  146.4 0.0 reduce-scatter.2.cloned.1.call-update
  146.5 1272.5 %reduce-scatter.2.cloned.1.call-done = f32[4,8,128]{2,1,0:T(8,128)} async-done(((f32[1024,8,128]{2,1,0:T(8,128)}), f32[4,8,128]{2,1,0:T(8,128)}) %reduce-scatter.2.cloned.1.call-update) | async-done | bytes 16400 | tf_op jit(solution)/shard_map/reduce_scatter | solution.py:49
  1419.0 0.9 convolution_bitcast_fusion
  1419.9 0.0 copy-done.1
  1419.9 0.9 convolution_bitcast_fusion.1
  1420.7 78.3 %all-reduce = (f32[8,8]{0,1:T(8,128)S(1)}, f32[8,8]{0,1:T(8,128)S(1)}) all-reduce(f32[8,8]{0,1:T(8,128)S(1)} %convolution_bitcast_fusion.1, f32[8,8]{0,1:T(8,128)S(1)} %convolution_bitcast_fusion), channel_id=1, replica_groups=mesh['tri'=256] {'tri'}, use_global_device_ids=true, to_apply=%region_5.6 | all-reduce | flops 128 | bytes 1024 | tf_op jit(solution)/shard_map/psum | solution.py:53
  1499.0 0.7 copy.12
  1499.7 0.7 copy.13
  (3 shorter events, 0.0 us)
Async XLA Ops:
  7.2 131.6 %copy-start.3 = (s32[32]{0:T(128)S(1)}, s32[32]{0:T(128)}, u32[]{:S(2)}) copy-start(s32[32]{0:T(128)} %param.9) | copy-start | bytes 388
  7.2 131.6 %copy-start.2 = (s32[32]{0:T(128)S(1)}, s32[32]{0:T(128)}, u32[]{:S(2)}) copy-start(s32[32]{0:T(128)} %param.8) | copy-start | bytes 388
  7.2 131.5 %copy-start = (f32[32,128,128]{2,1,0:T(8,128)S(1)}, f32[32,128,128]{2,1,0:T(8,128)}, u32[]{:S(2)}) copy-start(f32[32,128,128]{2,1,0:T(8,128)} %param.7) | copy-start | bytes 6291460
  7.2 123.8 %all-gather.2.cloned.1.call-start = ((), (), s32[]{:S(2)}) async-start(), calls=%async_computation.1 | async-start | bytes 4210688 | tf_op jit(solution)/shard_map/all_gather | solution.py:39
  7.9 1411.0 %reduce-scatter.2.cloned.1.call-start = ((), (), s32[]{:S(2)}) async-start(), calls=%async_computation.2 | async-start | bytes 4210688 | tf_op jit(solution)/shard_map/reduce_scatter | solution.py:49
  146.4 1273.4 %copy-start.1 = (f32[4,8,128]{2,1,0:T(8,128)S(1)}, f32[4,8,128]{2,1,0:T(8,128)}, u32[]{:S(2)}) copy-start(f32[4,8,128]{2,1,0:T(8,128)} %param.11) | copy-start | bytes 49156
Sparse Core Ops, SparseCore 0:
  11.6 119.3 all-gather.1
  146.6 1272.3 reduce-scatter.1
where the time goes:
time: 1510 us
  waiting for transfers between devices  1390 us (92%)
  blocking collectives  78.3 us (5%)
    reduce_scatter x1, waiting for transfers between devices, per_device(): image = lax.psum_scatter(totals, 'tri', scatter_dimension=0, tiled=True)  1270 us
    all_gather x1, waiting for transfers between devices, per_device(): gathered = lax.all_gather(block_vectors, 'tri', axis=0, tiled=True)  121 us
    psum x1, blocking collectives, per_device(): mixed_sum, image_sum = lax.psum((mixed_after, image_local), 'tri')  78.3 us
  transfers between devices with their start and end apart: 2, of which 2 were waited for; matrix products, arithmetic and copies ran while one was open for 0% of the time, Pallas kernels for 0%

commit v1 on v0

v1 whole, which is shorter than its diff:
```python
import jax
import jax.numpy as jnp
from jax import lax
from jax.experimental import pallas as pl
from jax.experimental.pallas import tpu as pltpu
from jax.sharding import PartitionSpec as P

MESH = pl.DeviceIdType.MESH
SEGS = 22
TILES = 1024
SHARE = 4
VEC = 8
WIDTH = 128
ROWS = SHARE * VEC
SLOTS = 32
WINDOW = 13
PAD = 64
BLOCKS = SEGS * (SEGS + 1) // 2
DEVICES = 256
NT_DIMS = (((1,), (1,)), ((), ()))
NN_DIMS = (((1,), (0,)), ((), ()))


def seg_low(s):
    return (s * TILES) // SEGS


def seg_of(t):
    return ((t + 1) * SEGS - 1) // TILES


def first_share(s):
    return seg_low(s) // SHARE


def shares(s):
    return (seg_low(s + 1) - 1) // SHARE - first_share(s) + 1


def block_of(d):
    row = 0
    for m in range(1, SEGS):
        row = row + jnp.where(d >= m * (m + 1) // 2, 1, 0)
    col = d - (row * (row + 1)) // 2
    return row, jnp.minimum(col, row)


def member(s, m):
    is_row = m <= s
    dev = jnp.where(is_row, (s * (s + 1)) // 2 + m, (m * (m + 1)) // 2 + s)
    return dev, is_row


def split(a):
    hi = a.astype(jnp.bfloat16)
    lo = (a - hi.astype(jnp.float32)).astype(jnp.bfloat16)
    return hi, lo


def kernel(
    tiles_ref, rows_ref, cols_ref, count_ref, rows_vec, cols_vec, x_ref,
    image_ref, grams_ref,
    tile_buf, hi_buf, lo_buf, xb, row_terms, col_terms, contrib, arrived,
    gram_own, gram_a, gram_b, gram_c,
    tile_sem, gather_send, gather_recv, scatter_send, scatter_recv, gram_send, gram_recv,
):
    me = lax.axis_index("tri")
    row, col = block_of(me)
    works = me < BLOCKS
    diagonal = row == col
    seg_a = seg_of(SHARE * me)
    seg_b = seg_of(SHARE * me + SHARE - 1)
    two = seg_b > seg_a

    tile_copy = pltpu.make_async_copy(tiles_ref, tile_buf, tile_sem)
    tile_copy.start()

    barrier = pltpu.get_barrier_semaphore()

    def greet(dev):
        pl.semaphore_signal(barrier, inc=1, device_id=(dev,), device_id_type=MESH)

    def greet_segment(s):
        def body(p, _):
            dev = first_share(s) + p

            @pl.when(dev != me)
            def _():
                greet(dev)

            return 0

        lax.fori_loop(0, shares(s), body, 0)

    @pl.when(works)
    def _():
        greet_segment(row)

        @pl.when(jnp.logical_not(diagonal))
        def _():
            greet_segment(col)

    base_a = (me // 8) * 8
    base_b = (me // 64) * 64 + me % 8
    base_c = me % 64
    groups = ((base_a, 1, 8), (base_b, 8, 8), (base_c, 64, 4))
    for base, stride, size in groups:
        for q in range(size):
            dev = base + q * stride

            @pl.when(dev != me)
            def _():
                greet(dev)

    def is_member(s):
        return jnp.logical_and(works, jnp.logical_or(row == s, col == s))

    expected = 17 + SEGS - jnp.where(is_member(seg_a), 1, 0)
    expected = expected + jnp.where(two, SEGS - jnp.where(is_member(seg_b), 1, 0), 0)
    pl.semaphore_wait(barrier, expected)

    def gather_copy(s, m, w):
        dev, is_row = member(s, m)
        which = jnp.where(is_row, 0, 1)
        dst = xb.at[which, pl.ds((me - first_share(s)) * SHARE, SHARE)]
        remote = pltpu.make_async_remote_copy(
            src_ref=x_ref, dst_ref=dst, send_sem=gather_send.at[w * SEGS + m],
            recv_sem=gather_recv.at[which], device_id=(dev,), device_id_type=MESH,
        )
        local = pltpu.make_async_copy(x_ref, dst, gather_recv.at[which])
        return dev, remote, local

    def gather_segment(s, w):
        def body(m, _):
            dev, remote, local = gather_copy(s, m, w)

            @pl.when(dev != me)
            def _():
                remote.start()

            @pl.when(dev == me)
            def _():
                local.start()

            return 0

        lax.fori_loop(0, SEGS, body, 0)

    gather_segment(seg_a, 0)

    @pl.when(two)
    def _():
        gather_segment(seg_b, 1)

    tile_copy.wait()

    def split_tile(k, _):
        hi, lo = split(tile_buf[k])
        hi_buf[k] = hi
        lo_buf[k] = lo
        return 0

    lax.fori_loop(0, SLOTS, split_tile, 0)

    def wait_rows(s, which):
        for n in (WINDOW - 1, WINDOW):
            @pl.when(shares(s) == n)
            def _():
                view = xb.at[which, pl.ds(0, n * SHARE)]
                pltpu.make_async_copy(view, view, gather_recv.at[which]).wait()

    @pl.when(works)
    def _():
        wait_rows(row, 0)

        @pl.when(jnp.logical_not(diagonal))
        def _():
            wait_rows(col, 1)

        row_base = SHARE * first_share(row)
        col_base = SHARE * first_share(col)
        col_which = jnp.where(diagonal, 0, 1)

        def operand(which, tile, base):
            hi, lo = split(xb[which, jnp.clip(tile - base, 0, WINDOW * SHARE - 1)])
            both = jnp.concatenate([hi, lo], axis=0)
            return jnp.concatenate([both, both], axis=1)

        def one_slot(k):
            x_col = operand(col_which, cols_ref[k], col_base)
            x_row = operand(0, rows_ref[k], row_base)
            hi, lo = hi_buf[k], lo_buf[k]
            by_row = lax.dot_general(
                x_col, jnp.concatenate([hi, lo], axis=1), NT_DIMS,
                preferred_element_type=jnp.float32,
            )
            by_col = lax.dot_general(
                x_row, jnp.concatenate([hi, lo], axis=0), NN_DIMS,
                preferred_element_type=jnp.float32,
            )
            at = pl.ds(pl.multiple_of(k * VEC, VEC), VEC)
            row_terms[at, :] = by_row[:VEC] + by_row[VEC:]
            col_terms[at, :] = by_col[:VEC] + by_col[VEC:]

        def four_slots(n, _):
            for u in range(4):
                one_slot(4 * n + u)
            return 0

        lax.fori_loop(0, SLOTS // 4, four_slots, 0)

        live = lax.broadcasted_iota(jnp.int32, (PAD, SLOTS), 1) < count_ref[0]
        place = lax.broadcasted_iota(jnp.int32, (PAD, SLOTS), 0)

        def chooser(vec, base):
            hit = jnp.logical_and(place == vec[...] - base, live)
            hot = hit.astype(jnp.float32).astype(jnp.bfloat16)
            return jnp.concatenate([hot, hot], axis=1)

        row_hot = chooser(rows_vec, row_base)
        col_hot = chooser(cols_vec, col_base)

        def reduced(hot, terms, v):
            hi, lo = split(terms[pl.ds(v, SLOTS, stride=VEC), :])
            return lax.dot_general(
                hot, jnp.concatenate([hi, lo], axis=0), NN_DIMS,
                preferred_element_type=jnp.float32,
            )

        for v in range(VEC):
            to_row = reduced(row_hot, row_terms, v)
            to_col = reduced(col_hot, col_terms, v)
            contrib[0, pl.ds(v, PAD, stride=VEC), :] = to_row + jnp.where(diagonal, to_col, 0.0)
            contrib[1, pl.ds(v, PAD, stride=VEC), :] = to_col

        def scatter_segment(s, which, m, start):
            def body(p, _):
                owner = first_share(s) + p
                second = jnp.where(seg_of(SHARE * owner) == s, 0, 1)
                src = contrib.at[which, pl.ds(pl.multiple_of(p * ROWS, ROWS), ROWS), :]
                dst = arrived.at[second, m]
                sem = scatter_recv.at[second]
                remote = pltpu.make_async_remote_copy(
                    src_ref=src, dst_ref=dst, send_sem=scatter_send.at[which * WINDOW + p],
                    recv_sem=sem, device_id=(owner,), device_id_type=MESH,
                )
                local = pltpu.make_async_copy(src, dst, sem)

                @pl.when(owner != me)
                def _():
                    if start:
                        remote.start()
                    else:
                        remote.wait_send()

                if start:
                    @pl.when(owner == me)
                    def _():
                        local.start()

                return 0

            lax.fori_loop(0, shares(s), body, 0)

        scatter_segment(row, 0, col, True)

        @pl.when(jnp.logical_not(diagonal))
        def _():
            scatter_segment(col, 1, row, True)

        scatter_segment(row, 0, col, False)

        @pl.when(jnp.logical_not(diagonal))
        def _():
            scatter_segment(col, 1, row, False)

    def collect(second, start):
        view = arrived.at[second]
        pltpu.make_async_copy(view, view, scatter_recv.at[second]).wait()
        return lax.fori_loop(0, SEGS, lambda m, acc: acc + arrived[second, m], start)

    def put(total):
        for t in range(SHARE):
            image_ref[t] = total[t * VEC:(t + 1) * VEC]

    put(collect(0, jnp.zeros((ROWS, WIDTH), jnp.float32)))

    @pl.when(two)
    def _():
        put(collect(1, jnp.concatenate([image_ref[t] for t in range(SHARE)], axis=0)))

    def flat(ref):
        return jnp.concatenate([ref[t] for t in range(SHARE)], axis=1)

    image = flat(image_ref)
    both = jnp.concatenate([flat(x_ref), image], axis=0)
    gram_own[0] = jnp.zeros((2 * VEC, WIDTH), jnp.float32)
    gram_own[0, :, 0:VEC] = lax.dot_general(
        both, image, NT_DIMS, precision=lax.Precision.HIGHEST, preferred_element_type=jnp.float32
    )

    for n, (buf, (base, stride, size)) in enumerate(zip((gram_a, gram_b, gram_c), groups)):
        rank = (me - base) // stride
        buf[rank] = gram_own[n]

        def swap(q, n=n, buf=buf, base=base, stride=stride, rank=rank):
            dev = base + q * stride
            return dev, pltpu.make_async_remote_copy(
                src_ref=gram_own.at[n], dst_ref=buf.at[rank], send_sem=gram_send.at[n * 8 + q],
                recv_sem=gram_recv.at[n], device_id=(dev,), device_id_type=MESH,
            )

        for q in range(size):
            dev, copy = swap(q)

            @pl.when(dev != me)
            def _():
                copy.start()

        view = buf.at[pl.ds(0, size - 1)]
        pltpu.make_async_copy(view, view, gram_recv.at[n]).wait()
        total = buf[0]
        for q in range(1, size):
            total = total + buf[q]
        if n < 2:
            gram_own[n + 1] = total
        else:
            grams_ref[...] = total * (1.0 / (TILES * WIDTH))
        for q in range(size):
            dev, copy = swap(q)

            @pl.when(dev != me)
            def _():
                copy.wait_send()

    def finish_segment(s, w):
        def body(m, _):
            dev, remote, _local = gather_copy(s, m, w)

            @pl.when(dev != me)
            def _():
                remote.wait_send()

            return 0

        lax.fori_loop(0, SEGS, body, 0)

    finish_segment(seg_a, 0)

    @pl.when(two)
    def _():
        finish_segment(seg_b, 1)


def per_device(tiles, tile_rows, tile_cols, counts, block_vectors):
    f32 = jnp.float32
    vmem = pl.BlockSpec(memory_space=pltpu.VMEM)
    smem = pl.BlockSpec(memory_space=pltpu.SMEM)
    image, grams = pl.pallas_call(
        kernel,
        out_shape=(
            jax.ShapeDtypeStruct((SHARE, VEC, WIDTH), f32),
            jax.ShapeDtypeStruct((2 * VEC, WIDTH), f32),
        ),
        in_specs=[pl.BlockSpec(memory_space=pl.ANY), smem, smem, smem, vmem, vmem, vmem],
        out_specs=(vmem, vmem),
        scratch_shapes=[
            pltpu.VMEM((SLOTS, WIDTH, WIDTH), f32),
            pltpu.VMEM((SLOTS, WIDTH, WIDTH), jnp.bfloat16),
            pltpu.VMEM((SLOTS, WIDTH, WIDTH), jnp.bfloat16),
            pltpu.VMEM((2, WINDOW * SHARE, VEC, WIDTH), f32),
            pltpu.VMEM((SLOTS * VEC, WIDTH), f32),
            pltpu.VMEM((SLOTS * VEC, WIDTH), f32),
            pltpu.VMEM((2, PAD * VEC, WIDTH), f32),
            pltpu.VMEM((2, SEGS, ROWS, WIDTH), f32),
            pltpu.VMEM((3, 2 * VEC, WIDTH), f32),
            pltpu.VMEM((8, 2 * VEC, WIDTH), f32),
            pltpu.VMEM((8, 2 * VEC, WIDTH), f32),
            pltpu.VMEM((4, 2 * VEC, WIDTH), f32),
            pltpu.SemaphoreType.DMA,
            pltpu.SemaphoreType.DMA((2 * SEGS,)),
            pltpu.SemaphoreType.DMA((2,)),
            pltpu.SemaphoreType.DMA((2 * WINDOW,)),
            pltpu.SemaphoreType.DMA((2,)),
            pltpu.SemaphoreType.DMA((24,)),
            pltpu.SemaphoreType.DMA((3,)),
        ],
        compiler_params=pltpu.CompilerParams(
            collective_id=0, has_side_effects=True, vmem_limit_bytes=32 * 1024 * 1024
        ),
    )(
        tiles, tile_rows, tile_cols, counts, tile_rows.reshape(1, SLOTS),
        tile_cols.reshape(1, SLOTS), block_vectors,
    )
    return image, grams[:VEC, :VEC], grams[VEC:, :VEC]


def solution(mesh):
    placed = (P("tri", None, None), P("tri"), P("tri"), P("tri"), P("tri", None, None))
    return jax.shard_map(
        per_device,
        mesh=mesh,
        in_specs=placed,
        out_specs=(P("tri", None, None), P(), P()),
        check_vma=False,
    )
```

time: 1510 us -> 70.7 us (0.05)
  waiting for transfers between devices: 1390 us -> 0 us
  blocking collectives: 78.3 us -> 0 us
  Pallas kernels: 0 us -> 63.7 us
    reduce_scatter x1 -> x0, waiting for transfers between devices: 1270 us -> none  [per_device(): image = lax.psum_scatter(totals, 'tri', scatter_dimension=0, tiled=True)]
    all_gather x1 -> x0, waiting for transfers between devices: 121 us -> none  [per_device(): gathered = lax.all_gather(block_vectors, 'tri', axis=0, tiled=True)]
    psum x1 -> x0, blocking collectives: 78.3 us -> none  [per_device(): mixed_sum, image_sum = lax.psum((mixed_after, image_local), 'tri')]
    pallas_call x0 -> x1, Pallas kernels: none -> 63.7 us  [per_device(): pl.pallas_call(kernel, out_shape=(jax.ShapeDtypeStruct((SHARE, VEC, WIDTH...]
  transfers between devices with their start and end apart: 2 -> 0, of which waited for: 2 -> 0; matrix products, arithmetic and copies ran while one was open for 0% -> 0% of each run, Pallas kernels for 0% -> 0%
where the time goes in v1:
time: 70.7 us; the launch traced here: 69.8 us
  Pallas kernels  63.7 us (90%)
  local copies, waits for them, and re-layouts  4.82 us (7%)
  between operations  1.3 us (2%)
    pallas_call x1, Pallas kernels, per_device(): pl.pallas_call(kernel, out_shape=(jax.ShapeDtypeStruct((SHARE, VEC, WIDTH...  63.7 us
    unnamed x9, local copies, waits for them, and re-layouts  4.22 us

profile of v1, /device:TPU:1, one launch (start us, length us, event | category | flops | bytes accessed | tf_op | source)
XLA Modules:
  0.0 69.8 jit_solution(6923210339948133555)
XLA Ops:
  1.3 0.0 copy-start
  1.3 1.6 %copy-done = f32[32,128,128]{2,1,0:T(8,128)S(1)} copy-done((f32[32,128,128]{2,1,0:T(8,128)S(1)}, f32[32,128,128]{2,1,0:T(8,128)}, u32[]{:S(2)}) %copy-start) | copy-done | bytes 2097176
  2.9 0.0 copy-start.1
  2.9 0.7 %copy-done.1 = f32[4,8,128]{2,1,0:T(8,128)S(1)} copy-done((f32[4,8,128]{2,1,0:T(8,128)S(1)}, f32[4,8,128]{2,1,0:T(8,128)}, u32[]{:S(2)}) %copy-start.1) | copy-done | bytes 16408
  3.6 0.0 copy-start.2
  3.6 0.7 copy-done.2
  4.2 0.0 copy-start.3
  4.2 0.7 copy-done.3
  4.9 63.7 %shard_map.76 = (f32[4,8,128]{2,1,0:T(8,128)S(1)}, f32[16,128]{1,0:T(8,128)S(1)}) custom-call(f32[32,128,128]{2,1,0:T(8,128)S(1)} %copy-done, s32[32]{0:T(128)S(1)} %copy-done.2, s32[32]{0:T(128)S(1)} %copy-done.3, s32[1]{0:T(128)S(6)} %copy.9.count_ref, s32[1,32]{1,0:T(1,128)S(1)} %bitcast.2, s32[1,32]{1,0:T(1,128)S(1)} %bitcast.3, f32[4,8,128]{2,1,0:T(8,128)S(1)} %copy-done.1), custom_call_target="tpu_custom_call" | custom-call | tf_op jit(solution)/shard_map/pallas_call | solution.py:359
  68.6 0.6 fusion
  69.2 0.6 copy.10
Async XLA Ops:
  1.3 1.6 %copy-start = (f32[32,128,128]{2,1,0:T(8,128)S(1)}, f32[32,128,128]{2,1,0:T(8,128)}, u32[]{:S(2)}) copy-start(f32[32,128,128]{2,1,0:T(8,128)} %tiles_ref.1) | copy-start | bytes 6291460
  2.9 0.7 %copy-start.1 = (f32[4,8,128]{2,1,0:T(8,128)S(1)}, f32[4,8,128]{2,1,0:T(8,128)}, u32[]{:S(2)}) copy-start(f32[4,8,128]{2,1,0:T(8,128)} %x_ref.1) | copy-start | bytes 49156
  3.6 0.7 copy-start.2
  4.2 0.7 copy-start.3

commit v2 on v0

v2 whole, which is shorter than its diff:
```python
import jax
import jax.numpy as jnp
from jax import lax
from jax.experimental import pallas as pl
from jax.experimental.pallas import tpu as pltpu
from jax.sharding import PartitionSpec as P

MESH = pl.DeviceIdType.MESH
SEGS = 22
TILES = 1024
SHARE = 4
VEC = 8
WIDTH = 128
ROWS = SHARE * VEC
SLOTS = 32
WINDOW = 13
PAD = 64
BLOCKS = SEGS * (SEGS + 1) // 2
GROUP = 8
CIRCLE = 16
KEYS = 4
NT_DIMS = (((1,), (1,)), ((), ()))
NN_DIMS = (((1,), (0,)), ((), ()))


def seg_low(s):
    return (s * TILES) // SEGS


def seg_of(t):
    return ((t + 1) * SEGS - 1) // TILES


def first_share(s):
    return seg_low(s) // SHARE


def shares(s):
    return (seg_low(s + 1) - 1) // SHARE - first_share(s) + 1


def tri(s):
    return (s * (s + 1)) // 2


def row_of(d):
    row = 0
    for m in range(1, SEGS):
        row = row + jnp.where(d >= m * (m + 1) // 2, 1, 0)
    return row


def first_group(s):
    return tri(s) // GROUP


def groups_of(s):
    return (tri(s) + s) // GROUP - first_group(s) + 1


def split(a):
    hi = a.astype(jnp.bfloat16)
    lo = (a - hi.astype(jnp.float32)).astype(jnp.bfloat16)
    return hi, lo


def kernel(
    tiles_ref, rows_hbm, cols_hbm, rows_hbm2, cols_hbm2, count_hbm, x_hbm,
    image_ref, grams_ref,
    tile_buf, hi_buf, lo_buf, x_ref, rows_ref, cols_ref, rows_vec, cols_vec, count_ref,
    x_row, x_col, relay_buf, row_terms, col_terms, contrib, part_buf, part_sum, arrived,
    gram_own, gram_a, gram_b,
    in_sem, relay_send, relay_recv, pass_send, gather_send, gather_recv,
    part_send, part_recv, sum_send, col_send, arrive_recv, gram_send, gram_recv,
):
    me = lax.axis_index("tri")
    residue = me % GROUP
    group = me // GROUP
    base = group * GROUP
    works = me < BLOCKS
    row = row_of(me)
    col = jnp.minimum(me - tri(row), row)
    off_diagonal = jnp.logical_and(works, row > col)
    on_diagonal = jnp.logical_and(works, row == col)
    top = row_of(base)
    rows_here = row_of(jnp.minimum(base + GROUP - 1, BLOCKS - 1)) - top + 1
    seg_a = seg_of(SHARE * me)
    seg_b = seg_of(SHARE * me + SHARE - 1)
    two = seg_b > seg_a

    loads = [
        pltpu.make_async_copy(src, dst, in_sem.at[n])
        for n, (src, dst) in enumerate((
            (x_hbm, x_ref), (tiles_ref, tile_buf), (rows_hbm, rows_ref), (cols_hbm, cols_ref),
            (rows_hbm2, rows_vec), (cols_hbm2, cols_vec), (count_hbm, count_ref),
        ))
    ]
    for load in loads:
        load.start()

    def loop(n, body):
        def step(i, _):
            body(i)
            return 0

        lax.fori_loop(0, n, step, 0)

    def owned(body):
        body(seg_a, 0)

        @pl.when(two)
        def _():
            body(seg_b, 1)

    def relayed(body):
        def each(n):
            s = top + n
            start = (residue - first_share(s) % GROUP + GROUP) % GROUP
            for turn in range(2):
                p = start + GROUP * turn

                @pl.when(p < shares(s))
                def _():
                    body(s, p, s % KEYS, turn)

        loop(rows_here, each)

    def members(s, body):
        low = jnp.maximum(tri(s), base)
        high = jnp.minimum(tri(s) + s, base + GROUP - 1)
        loop(high - low + 1, lambda i: body(low + i))

    def send(src, dst, send_sem, recv_sem, dev):
        @pl.when(dev != me)
        def _():
            pltpu.make_async_remote_copy(
                src_ref=src, dst_ref=dst, send_sem=send_sem, recv_sem=recv_sem,
                device_id=(dev,), device_id_type=MESH,
            ).start()

        @pl.when(dev == me)
        def _():
            pltpu.make_async_copy(src, dst, recv_sem).start()

    def sent(src, send_sem, dev):
        @pl.when(dev != me)
        def _():
            pltpu.make_async_copy(src, src, send_sem).wait()

    def landed(dst, recv_sem):
        pltpu.make_async_copy(dst, dst, recv_sem).wait()

    barrier = pltpu.get_barrier_semaphore()

    def greet(dev):
        @pl.when(dev != me)
        def _():
            pl.semaphore_signal(barrier, inc=1, device_id=(dev,), device_id_type=MESH)

    @pl.when(off_diagonal)
    def _():
        loop(shares(col), lambda p: greet(first_share(col) + p))

    relayed(lambda s, p, key, turn: greet(first_share(s) + p))

    core, x, z, y = me % 2, residue // 2, group % 8, me // 64

    def device(y, z, x, core):
        return ((y * 8 + z) * 4 + x) * 2 + core

    for q in range(GROUP):
        greet(base + q)
    for dz in range(1, 8):
        for q in range(2):
            greet(device(y, (z + dz) % 8, x, q))
    for dy in range(1, 4):
        for q in range(4):
            greet(device((y + dy) % 4, z, q, core))

    def greeters(s):
        mine = jnp.logical_and(group >= first_group(s), group < first_group(s) + groups_of(s))
        n = groups_of(s) - jnp.where(mine, 1, 0)
        return n + SEGS - 1 - s - jnp.where(jnp.logical_and(off_diagonal, col == s), 1, 0)

    pl.semaphore_wait(barrier, 33 + greeters(seg_a) + jnp.where(two, greeters(seg_b), 0))
    loads[0].wait()

    def to_relays(start):
        def body(s, w):
            turn = (me - first_share(s)) // GROUP
            dst, sem = relay_buf.at[s % KEYS, turn], relay_recv.at[s % KEYS, turn]

            def each(n):
                dev = (first_group(s) + n) * GROUP + residue
                if start:
                    send(x_ref, dst, relay_send.at[w * KEYS + n], sem, dev)
                else:
                    sent(x_ref, relay_send.at[w * KEYS + n], dev)

            loop(groups_of(s), each)

        return body

    def to_columns(start):
        def body(s, w):
            dst = x_col.at[pl.ds((me - first_share(s)) * SHARE, SHARE)]

            def each(n):
                dev = tri(s + 1 + n) + s
                if start:
                    send(x_ref, dst, gather_send.at[w * SEGS + n], gather_recv.at[1], dev)
                else:
                    sent(x_ref, gather_send.at[w * SEGS + n], dev)

            loop(SEGS - 1 - s, each)

        return body

    owned(to_relays(True))
    owned(to_columns(True))

    for load in loads[1:]:
        load.wait()

    def split_tile(k):
        hi, lo = split(tile_buf[k])
        hi_buf[k] = hi
        lo_buf[k] = lo

    loop(SLOTS, split_tile)

    def pass_on(start):
        def body(s, p, key, turn):
            src = relay_buf.at[key, turn]
            dst = x_row.at[pl.ds(p * SHARE, SHARE)]
            if start:
                landed(src, relay_recv.at[key, turn])

            def each(dev):
                sem = pass_send.at[key, turn, dev % GROUP]
                if start:
                    send(src, dst, sem, gather_recv.at[0], dev)
                else:
                    sent(src, sem, dev)

            members(s, each)

        return body

    relayed(pass_on(True))

    def wait_rows(s, held, recv_sem):
        for n in (WINDOW - 1, WINDOW):
            @pl.when(shares(s) == n)
            def _():
                landed(held.at[pl.ds(0, n * SHARE)], recv_sem)

    def wait_row():
        wait_rows(row, x_row, gather_recv.at[0])

    row_base = SHARE * first_share(row)
    col_base = SHARE * first_share(col)

    def multiply(held, ids, origin, terms, axis, dims):
        def one(k):
            hi, lo = split(held[jnp.clip(ids[k] - origin, 0, WINDOW * SHARE - 1)])
            both = jnp.concatenate([hi, lo], axis=0)
            out = lax.dot_general(
                jnp.concatenate([both, both], axis=1),
                jnp.concatenate([hi_buf[k], lo_buf[k]], axis=axis), dims,
                preferred_element_type=jnp.float32,
            )
            terms[pl.ds(pl.multiple_of(k * VEC, VEC), VEC), :] = out[:VEC] + out[VEC:]

        def several(n):
            for u in range(8):
                one(8 * n + u)

        loop(SLOTS // 8, several)

    def reduce(vec, origin, terms, which):
        live = lax.broadcasted_iota(jnp.int32, (PAD, SLOTS), 1) < count_ref[0]
        place = lax.broadcasted_iota(jnp.int32, (PAD, SLOTS), 0)
        hit = jnp.logical_and(place == vec[...] - origin, live)
        hot = hit.astype(jnp.float32).astype(jnp.bfloat16)
        hot = jnp.concatenate([hot, hot], axis=1)
        for v in range(VEC):
            hi, lo = split(terms[pl.ds(v, SLOTS, stride=VEC), :])
            contrib[which, pl.ds(v, PAD, stride=VEC), :] = lax.dot_general(
                hot, jnp.concatenate([hi, lo], axis=0), NN_DIMS,
                preferred_element_type=jnp.float32,
            )

    def chunk(which, p):
        return contrib.at[which, pl.ds(pl.multiple_of(p * ROWS, ROWS), ROWS), :]

    def row_parts(start):
        def each(p):
            dev = base + (first_share(row) + p) % GROUP
            if start:
                turn = p // GROUP
                send(
                    chunk(0, p), part_buf.at[row % KEYS, turn, residue], part_send.at[p],
                    part_recv.at[row % KEYS, turn, residue], dev,
                )
            else:
                sent(chunk(0, p), part_send.at[p], dev)

        loop(shares(row), each)

    def place_of(owner, s):
        return jnp.where(seg_of(SHARE * owner) == s, 0, 1)

    def col_parts(start):
        def each(p):
            owner = first_share(col) + p
            if start:
                second = place_of(owner, col)
                send(
                    chunk(1, p), arrived.at[second, KEYS + row], col_send.at[p],
                    arrive_recv.at[second, KEYS + row], owner,
                )
            else:
                sent(chunk(1, p), col_send.at[p], owner)

        loop(shares(col), each)

    @pl.when(works)
    def _():
        @pl.when(off_diagonal)
        def _():
            wait_rows(col, x_col, gather_recv.at[1])
            multiply(x_col, cols_ref, col_base, row_terms, 1, NT_DIMS)

        @pl.when(on_diagonal)
        def _():
            wait_row()
            multiply(x_row, cols_ref, col_base, row_terms, 1, NT_DIMS)

        reduce(rows_vec, row_base, row_terms, 0)

        @pl.when(off_diagonal)
        def _():
            row_parts(True)
            wait_row()

        multiply(x_row, rows_ref, row_base, col_terms, 0, NN_DIMS)
        reduce(cols_vec, col_base, col_terms, 1)

        @pl.when(off_diagonal)
        def _():
            col_parts(True)

        @pl.when(on_diagonal)
        def _():
            contrib[0] = contrib[0] + contrib[1]
            row_parts(True)

    owned(to_relays(False))
    owned(to_columns(False))
    relayed(pass_on(False))

    def add_parts(start):
        def body(s, p, key, turn):
            owner = first_share(s) + p
            src = part_sum.at[key, turn]
            if start:
                low = jnp.maximum(tri(s), base)
                high = jnp.minimum(tri(s) + s, base + GROUP - 1)

                def each(i, total):
                    rank = (low + i) % GROUP
                    landed(part_buf.at[key, turn, rank], part_recv.at[key, turn, rank])
                    return total + part_buf[key, turn, rank]

                part_sum[key, turn] = lax.fori_loop(
                    0, high - low + 1, each, jnp.zeros((ROWS, WIDTH), jnp.float32)
                )
                second = place_of(owner, s)
                at = group - first_group(s)
                send(
                    src, arrived.at[second, at], sum_send.at[key, turn],
                    arrive_recv.at[second, at], owner,
                )
            else:
                sent(src, sum_send.at[key, turn], owner)

        return body

    relayed(add_parts(True))

    def collect(w, s, total):
        def each(at, total):
            landed(arrived.at[w, at], arrive_recv.at[w, at])
            return total + arrived[w, at]

        total = lax.fori_loop(KEYS + s + 1, KEYS + SEGS, each, total)
        return lax.fori_loop(0, groups_of(s), each, total)

    def put(total):
        for t in range(SHARE):
            image_ref[t] = total[t * VEC:(t + 1) * VEC]

    put(collect(0, seg_a, jnp.zeros((ROWS, WIDTH), jnp.float32)))

    @pl.when(two)
    def _():
        put(collect(1, seg_b, jnp.concatenate([image_ref[t] for t in range(SHARE)], axis=0)))

    def flat(ref):
        return jnp.concatenate([ref[t] for t in range(SHARE)], axis=1)

    image = flat(image_ref)
    both = lax.dot_general(
        jnp.concatenate([flat(x_ref), image], axis=0), image, NT_DIMS,
        precision=lax.Precision.HIGHEST, preferred_element_type=jnp.float32,
    )
    gram_own[0] = jnp.zeros((VEC, WIDTH), jnp.float32)
    gram_own[0, :, 0:VEC] = both[:VEC]
    gram_own[0, :, VEC:2 * VEC] = both[VEC:]

    circles = (
        (gram_a, z * 2 + core, lambda q: device(y, q // 2, x, q % 2)),
        (gram_b, y * 4 + x, lambda q: device(q // 4, z, q % 4, core)),
    )
    for n, (buf, rank, partner) in enumerate(circles):
        for q in range(CIRCLE):
            @pl.when(q != rank)
            def _():
                pltpu.make_async_remote_copy(
                    src_ref=gram_own.at[n], dst_ref=buf.at[rank], send_sem=gram_send.at[n, q],
                    recv_sem=gram_recv.at[n], device_id=(partner(q),), device_id_type=MESH,
                ).start()

        buf[rank] = gram_own[n]
        if n == 0:
            relayed(add_parts(False))

            @pl.when(works)
            def _():
                row_parts(False)

            @pl.when(off_diagonal)
            def _():
                col_parts(False)

        landed(buf.at[pl.ds(0, CIRCLE - 1)], gram_recv.at[n])
        terms = [buf[q] for q in range(CIRCLE)]
        while len(terms) > 1:
            terms = [a + b for a, b in zip(terms[::2], terms[1::2])]
        if n == 0:
            gram_own[1] = terms[0]
        else:
            grams_ref[...] = terms[0] * (1.0 / (TILES * WIDTH))

    for n, (_buf, rank, _partner) in enumerate(circles):
        for q in range(CIRCLE):
            @pl.when(q != rank)
            def _():
                pltpu.make_async_copy(gram_own.at[n], gram_own.at[n], gram_send.at[n, q]).wait()


def per_device(tiles, tile_rows, tile_cols, counts, block_vectors):
    f32, i32 = jnp.float32, jnp.int32
    vmem = pl.BlockSpec(memory_space=pltpu.VMEM)
    dma = pltpu.SemaphoreType.DMA
    image, grams = pl.pallas_call(
        kernel,
        out_shape=(
            jax.ShapeDtypeStruct((SHARE, VEC, WIDTH), f32),
            jax.ShapeDtypeStruct((VEC, WIDTH), f32),
        ),
        in_specs=[pl.BlockSpec(memory_space=pl.ANY)] * 7,
        out_specs=(vmem, vmem),
        scratch_shapes=[
            pltpu.VMEM((SLOTS, WIDTH, WIDTH), f32),
            pltpu.VMEM((SLOTS, WIDTH, WIDTH), jnp.bfloat16),
            pltpu.VMEM((SLOTS, WIDTH, WIDTH), jnp.bfloat16),
            pltpu.VMEM((SHARE, VEC, WIDTH), f32),
            pltpu.SMEM((SLOTS,), i32),
            pltpu.SMEM((SLOTS,), i32),
            pltpu.VMEM((1, SLOTS), i32),
            pltpu.VMEM((1, SLOTS), i32),
            pltpu.SMEM((1,), i32),
            pltpu.VMEM((WINDOW * SHARE, VEC, WIDTH), f32),
            pltpu.VMEM((WINDOW * SHARE, VEC, WIDTH), f32),
            pltpu.VMEM((KEYS, 2, SHARE, VEC, WIDTH), f32),
            pltpu.VMEM((SLOTS * VEC, WIDTH), f32),
            pltpu.VMEM((SLOTS * VEC, WIDTH), f32),
            pltpu.VMEM((2, PAD * VEC, WIDTH), f32),
            pltpu.VMEM((KEYS, 2, GROUP, ROWS, WIDTH), f32),
            pltpu.VMEM((KEYS, 2, ROWS, WIDTH), f32),
            pltpu.VMEM((2, KEYS + SEGS, ROWS, WIDTH), f32),
            pltpu.VMEM((2, VEC, WIDTH), f32),
            pltpu.VMEM((CIRCLE, VEC, WIDTH), f32),
            pltpu.VMEM((CIRCLE, VEC, WIDTH), f32),
            dma((7,)),
            dma((2 * KEYS,)),
            dma((KEYS, 2)),
            dma((KEYS, 2, GROUP)),
            dma((2 * SEGS,)),
            dma((2,)),
            dma((WINDOW,)),
            dma((KEYS, 2, GROUP)),
            dma((KEYS, 2)),
            dma((WINDOW,)),
            dma((2, KEYS + SEGS)),
            dma((2, CIRCLE)),
            dma((2,)),
        ],
        compiler_params=pltpu.CompilerParams(
            collective_id=0, has_side_effects=True, vmem_limit_bytes=60 * 1024 * 1024
        ),
    )(
        tiles, tile_rows, tile_cols, tile_rows.reshape(1, SLOTS), tile_cols.reshape(1, SLOTS),
        counts, block_vectors,
    )
    return image, grams[:, :VEC], grams[:, VEC:2 * VEC]


def solution(mesh):
    placed = (P("tri", None, None), P("tri"), P("tri"), P("tri"), P("tri", None, None))
    return jax.shard_map(
        per_device,
        mesh=mesh,
        in_specs=placed,
        out_specs=(P("tri", None, None), P(), P()),
        check_vma=False,
    )
```

time: 1510 us -> 54.6 us (0.04)
  waiting for transfers between devices: 1390 us -> 0 us
  blocking collectives: 78.3 us -> 0 us
  Pallas kernels: 0 us -> 50.3 us
    reduce_scatter x1 -> x0, waiting for transfers between devices: 1270 us -> none  [per_device(): image = lax.psum_scatter(totals, 'tri', scatter_dimension=0, tiled=True)]
    all_gather x1 -> x0, waiting for transfers between devices: 121 us -> none  [per_device(): gathered = lax.all_gather(block_vectors, 'tri', axis=0, tiled=True)]
    psum x1 -> x0, blocking collectives: 78.3 us -> none  [per_device(): mixed_sum, image_sum = lax.psum((mixed_after, image_local), 'tri')]
    pallas_call x0 -> x1, Pallas kernels: none -> 50.3 us  [per_device(): pl.pallas_call(kernel, out_shape=(jax.ShapeDtypeStruct((SHARE, VEC, WIDTH...]
  transfers between devices with their start and end apart: 2 -> 0, of which waited for: 2 -> 0; matrix products, arithmetic and copies ran while one was open for 0% -> 0% of each run, Pallas kernels for 0% -> 0%
where the time goes in v2:
time: 54.6 us; the launch traced here: 54.3 us
  Pallas kernels  50.3 us (92%)
  local copies, waits for them, and re-layouts  2.74 us (5%)
  between operations  1.29 us (2%)
    pallas_call x1, Pallas kernels, per_device(): pl.pallas_call(kernel, out_shape=(jax.ShapeDtypeStruct((SHARE, VEC, WIDTH...  50.3 us
    slice x1, local copies, waits for them, and re-layouts, per_device(): return (image, grams[:, :VEC], grams[:, VEC:2 * VEC])  1.42 us
    unnamed x1, local copies, waits for them, and re-layouts  1.32 us

profile of v2, /device:TPU:1, one launch (start us, length us, event | category | flops | bytes accessed | tf_op | source)
XLA Modules:
  0.0 54.3 jit_solution(14327637424099822415)
XLA Ops:
  1.3 50.3 %shard_map.76 = (f32[4,8,128]{2,1,0:T(8,128)}, f32[8,128]{1,0:T(8,128)}) custom-call(f32[32,128,128]{2,1,0:T(8,128)} %tiles_ref.1, s32[32]{0:T(128)} %rows_hbm.1, s32[32]{0:T(128)} %cols_hbm.1, s32[1,32]{1,0:T(1,128)} %bitcast.2, s32[1,32]{1,0:T(1,128)} %bitcast.3, s32[1]{0:T(128)S(6)} %copy.9.count_hbm, f32[4,8,128]{2,1,0:T(8,128)} %x_hbm.1), custom_call_target="tpu_custom_call" | custom-call | tf_op jit(solution)/shard_map/pallas_call | solution.py:467
  51.6 1.4 %fusion = (f32[8,8]{1,0:T(8,128)}, f32[8,8]{1,0:T(8,128)}) fusion(f32[8,128]{1,0:T(8,128)} %get-tuple-element.6), kind=kLoop, calls=%fused_computation | loop fusion | bytes 1024 | tf_op jit(solution)/shard_map/slice | solution.py:518
  53.0 1.3 %copy.10 = f32[4,8,128]{2,1,0:T(8,128)} copy(f32[4,8,128]{2,1,0:T(8,128)} %get-tuple-element.12) | data formatting | bytes 32768

commit v3 on v2

--- a/solution.py
+++ b/solution.py
@@ -55,7 +55,7 @@
 
 
 def groups_of(s):
-    return (tri(s) + s) // GROUP - first_group(s) + 1
+    return (tri(s) + s - 1) // GROUP - first_group(s) + 1
 
 
 def split(a):
@@ -95,8 +95,7 @@
             (rows_hbm2, rows_vec), (cols_hbm2, cols_vec), (count_hbm, count_ref),
         ))
     ]
-    for load in loads:
-        load.start()
+    loads[0].start()
 
     def loop(n, body):
         def step(i, _):
@@ -111,6 +110,10 @@
         @pl.when(two)
         def _():
             body(seg_b, 1)
+
+    def span(s):
+        low = jnp.maximum(tri(s), base)
+        return low, jnp.minimum(tri(s) + s, base + GROUP) - low
 
     def relayed(body):
         def each(n):
@@ -119,16 +122,15 @@
             for turn in range(2):
                 p = start + GROUP * turn
 
-                @pl.when(p < shares(s))
+                @pl.when(jnp.logical_and(p < shares(s), span(s)[1] > 0))
                 def _():
                     body(s, p, s % KEYS, turn)
 
         loop(rows_here, each)
 
     def members(s, body):
-        low = jnp.maximum(tri(s), base)
-        high = jnp.minimum(tri(s) + s, base + GROUP - 1)
-        loop(high - low + 1, lambda i: body(low + i))
+        low, count = span(s)
+        loop(count, lambda i: body(low + i))
 
     def send(src, dst, send_sem, recv_sem, dev):
         @pl.when(dev != me)
@@ -157,7 +159,7 @@
         def _():
             pl.semaphore_signal(barrier, inc=1, device_id=(dev,), device_id_type=MESH)
 
-    @pl.when(off_diagonal)
+    @pl.when(works)
     def _():
         loop(shares(col), lambda p: greet(first_share(col) + p))
 
@@ -177,10 +179,13 @@
         for q in range(4):
             greet(device((y + dy) % 4, z, q, core))
 
+    for load in loads[1:]:
+        load.start()
+
     def greeters(s):
         mine = jnp.logical_and(group >= first_group(s), group < first_group(s) + groups_of(s))
         n = groups_of(s) - jnp.where(mine, 1, 0)
-        return n + SEGS - 1 - s - jnp.where(jnp.logical_and(off_diagonal, col == s), 1, 0)
+        return n + SEGS - s - jnp.where(jnp.logical_and(works, col == s), 1, 0)
 
     pl.semaphore_wait(barrier, 33 + greeters(seg_a) + jnp.where(two, greeters(seg_b), 0))
     loads[0].wait()
@@ -206,13 +211,13 @@
             dst = x_col.at[pl.ds((me - first_share(s)) * SHARE, SHARE)]
 
             def each(n):
-                dev = tri(s + 1 + n) + s
+                dev = tri(s + n) + s
                 if start:
                     send(x_ref, dst, gather_send.at[w * SEGS + n], gather_recv.at[1], dev)
                 else:
                     sent(x_ref, gather_send.at[w * SEGS + n], dev)
 
-            loop(SEGS - 1 - s, each)
+            loop(SEGS - s, each)
 
         return body
 
@@ -254,9 +259,6 @@
             @pl.when(shares(s) == n)
             def _():
                 landed(held.at[pl.ds(0, n * SHARE)], recv_sem)
-
-    def wait_row():
-        wait_rows(row, x_row, gather_recv.at[0])
 
     row_base = SHARE * first_share(row)
     col_base = SHARE * first_share(col)
@@ -327,34 +329,27 @@
 
     @pl.when(works)
     def _():
+        wait_rows(col, x_col, gather_recv.at[1])
+        multiply(x_col, cols_ref, col_base, row_terms, 1, NT_DIMS)
+        reduce(rows_vec, row_base, row_terms, 0)
+
         @pl.when(off_diagonal)
         def _():
-            wait_rows(col, x_col, gather_recv.at[1])
-            multiply(x_col, cols_ref, col_base, row_terms, 1, NT_DIMS)
+            row_parts(True)
+            wait_rows(row, x_row, gather_recv.at[0])
+            multiply(x_row, rows_ref, row_base, col_terms, 0, NN_DIMS)
 
         @pl.when(on_diagonal)
         def _():
-            wait_row()
-            multiply(x_row, cols_ref, col_base, row_terms, 1, NT_DIMS)
-
-        reduce(rows_vec, row_base, row_terms, 0)
-
-        @pl.when(off_diagonal)
-        def _():
-            row_parts(True)
-            wait_row()
-
-        multiply(x_row, rows_ref, row_base, col_terms, 0, NN_DIMS)
+            multiply(x_col, rows_ref, row_base, col_terms, 0, NN_DIMS)
+
         reduce(cols_vec, col_base, col_terms, 1)
 
-        @pl.when(off_diagonal)
-        def _():
-            col_parts(True)
-
         @pl.when(on_diagonal)
         def _():
-            contrib[0] = contrib[0] + contrib[1]
-            row_parts(True)
+            contrib[1] = contrib[0] + contrib[1]
+
+        col_parts(True)
 
     owned(to_relays(False))
     owned(to_columns(False))
@@ -365,8 +360,7 @@
             owner = first_share(s) + p
             src = part_sum.at[key, turn]
             if start:
-                low = jnp.maximum(tri(s), base)
-                high = jnp.minimum(tri(s) + s, base + GROUP - 1)
+                low, count = span(s)
 
                 def each(i, total):
                     rank = (low + i) % GROUP
@@ -374,7 +368,7 @@
                     return total + part_buf[key, turn, rank]
 
                 part_sum[key, turn] = lax.fori_loop(
-                    0, high - low + 1, each, jnp.zeros((ROWS, WIDTH), jnp.float32)
+                    0, count, each, jnp.zeros((ROWS, WIDTH), jnp.float32)
                 )
                 second = place_of(owner, s)
                 at = group - first_group(s)
@@ -394,7 +388,7 @@
             landed(arrived.at[w, at], arrive_recv.at[w, at])
             return total + arrived[w, at]
 
-        total = lax.fori_loop(KEYS + s + 1, KEYS + SEGS, each, total)
+        total = lax.fori_loop(KEYS + s, KEYS + SEGS, each, total)
         return lax.fori_loop(0, groups_of(s), each, total)
 
     def put(total):
@@ -436,11 +430,11 @@
         if n == 0:
             relayed(add_parts(False))
 
-            @pl.when(works)
+            @pl.when(off_diagonal)
             def _():
                 row_parts(False)
 
-            @pl.when(off_diagonal)
+            @pl.when(works)
             def _():
                 col_parts(False)
 
@@ -467,8 +461,8 @@
     image, grams = pl.pallas_call(
         kernel,
         out_shape=(
-            jax.ShapeDtypeStruct((SHARE, VEC, WIDTH), f32),
-            jax.ShapeDtypeStruct((VEC, WIDTH), f32),
+            pltpu.VMEM((SHARE, VEC, WIDTH), f32),
+            pltpu.VMEM((VEC, WIDTH), f32),
         ),
         in_specs=[pl.BlockSpec(memory_space=pl.ANY)] * 7,
         out_specs=(vmem, vmem),

time: 54.6 us -> 53.7 us (0.984)
  local copies, waits for them, and re-layouts: 2.74 us -> 1.27 us
  Pallas kernels: 50.3 us -> 51 us
    slice x1, local copies, waits for them, and re-layouts: 1.42 us -> 0.66 us  [per_device(): return (image, grams[:, :VEC], grams[:, VEC:2 * VEC])]
    unnamed x1, local copies, waits for them, and re-layouts: 1.32 us -> 0.61 us
    pallas_call x1, Pallas kernels: 50.3 us -> 51 us  [per_device(): pl.pallas_call(kernel, out_shape=(pltpu.VMEM((SHARE, VEC, WIDTH), f32), p...]
where the time goes in v3:
time: 53.7 us; the launch traced here: 53.6 us
  Pallas kernels  51 us (95%)
  between operations  1.29 us (2%)
  local copies, waits for them, and re-layouts  1.27 us (2%)
    pallas_call x1, Pallas kernels, per_device(): pl.pallas_call(kernel, out_shape=(pltpu.VMEM((SHARE, VEC, WIDTH), f32), p...  51 us

profile of v3, /device:TPU:1, one launch (start us, length us, event | category | flops | bytes accessed | tf_op | source)
XLA Modules:
  0.0 53.6 jit_solution(11154907984356578413)
XLA Ops:
  1.3 51.0 %shard_map.76 = (f32[4,8,128]{2,1,0:T(8,128)S(1)}, f32[8,128]{1,0:T(8,128)S(1)}) custom-call(f32[32,128,128]{2,1,0:T(8,128)} %tiles_ref.1, s32[32]{0:T(128)} %rows_hbm.1, s32[32]{0:T(128)} %cols_hbm.1, s32[1,32]{1,0:T(1,128)} %bitcast.2, s32[1,32]{1,0:T(1,128)} %bitcast.3, s32[1]{0:T(128)S(6)} %copy.10.count_hbm, f32[4,8,128]{2,1,0:T(8,128)} %x_hbm.1), custom_call_target="tpu_custom_call" | custom-call | tf_op jit(solution)/shard_map/pallas_call | solution.py:461
  52.3 0.6 %copy.9 = f32[4,8,128]{2,1,0:T(8,128)} copy(f32[4,8,128]{2,1,0:T(8,128)S(1)} %get-tuple-element.9) | data formatting | bytes 32768
  52.9 0.7 %fusion = (f32[8,8]{1,0:T(8,128)}, f32[8,8]{1,0:T(8,128)}) fusion(f32[8,128]{1,0:T(8,128)S(1)} %get-tuple-element.6), kind=kLoop, calls=%fused_computation | loop fusion | bytes 1024 | tf_op jit(solution)/shard_map/slice | solution.py:512

commit v4 on v3

--- a/solution.py
+++ b/solution.py
@@ -17,7 +17,8 @@
 PAD = 64
 BLOCKS = SEGS * (SEGS + 1) // 2
 GROUP = 8
-CIRCLE = 16
+LINE = 8
+PLANE = 32
 KEYS = 4
 NT_DIMS = (((1,), (1,)), ((), ()))
 NN_DIMS = (((1,), (0,)), ((), ()))
@@ -68,10 +69,10 @@
     tiles_ref, rows_hbm, cols_hbm, rows_hbm2, cols_hbm2, count_hbm, x_hbm,
     image_ref, grams_ref,
     tile_buf, hi_buf, lo_buf, x_ref, rows_ref, cols_ref, rows_vec, cols_vec, count_ref,
-    x_row, x_col, relay_buf, row_terms, col_terms, contrib, part_buf, part_sum, arrived,
+    x_row, x_col, relay_buf, line_buf, col_buf, col_sum, row_terms, col_terms, contrib, part_buf, part_sum, arrived,
     gram_own, gram_a, gram_b,
-    in_sem, relay_send, relay_recv, pass_send, gather_send, gather_recv,
-    part_send, part_recv, sum_send, col_send, arrive_recv, gram_send, gram_recv,
+    in_sem, relay_send, relay_recv, pass_send, line_send, line_recv, spread_send, gather_recv,
+    part_send, part_recv, sum_send, col_send, col_recv, back_send, arrive_recv, gram_send, gram_recv,
 ):
     me = lax.axis_index("tri")
     residue = me % GROUP
@@ -159,36 +160,83 @@
         def _():
             pl.semaphore_signal(barrier, inc=1, device_id=(dev,), device_id_type=MESH)
 
-    @pl.when(works)
-    def _():
-        loop(shares(col), lambda p: greet(first_share(col) + p))
-
+    core, x, z, y = me % 2, residue // 2, group % LINE, me // 64
+
+    def line(zz):
+        return (y * LINE + zz) * GROUP + residue
+
+    def plane(q):
+        return (q // GROUP * LINE + z) * GROUP + q % GROUP
+
+    for dz in range(1, LINE):
+        greet(line((z + dz) % LINE))
+    for q in range(PLANE):
+        greet(plane(q))
     relayed(lambda s, p, key, turn: greet(first_share(s) + p))
-
-    core, x, z, y = me % 2, residue // 2, group % 8, me // 64
-
-    def device(y, z, x, core):
-        return ((y * 8 + z) * 4 + x) * 2 + core
-
-    for q in range(GROUP):
-        greet(base + q)
-    for dz in range(1, 8):
-        for q in range(2):
-            greet(device(y, (z + dz) % 8, x, q))
-    for dy in range(1, 4):
-        for q in range(4):
-            greet(device((y + dy) % 4, z, q, core))
 
     for load in loads[1:]:
         load.start()
 
     def greeters(s):
         mine = jnp.logical_and(group >= first_group(s), group < first_group(s) + groups_of(s))
-        n = groups_of(s) - jnp.where(mine, 1, 0)
-        return n + SEGS - s - jnp.where(jnp.logical_and(works, col == s), 1, 0)
-
-    pl.semaphore_wait(barrier, 33 + greeters(seg_a) + jnp.where(two, greeters(seg_b), 0))
+        return groups_of(s) - jnp.where(mine, 1, 0)
+
+    pl.semaphore_wait(barrier, LINE + PLANE - 2 + greeters(seg_a) + jnp.where(two, greeters(seg_b), 0))
     loads[0].wait()
+
+    def near_first(n):
+        return (z + jnp.where(n % 2 == 1, (n + 1) // 2, LINE - n // 2)) % LINE
+
+    def targets(zz, body):
+        owner = line(zz)
+        a, b = seg_of(SHARE * owner), seg_of(SHARE * owner + SHARE - 1)
+
+        def one(s, w):
+            p = owner - first_share(s)
+
+            def each(n):
+                k = s + n
+                dev = tri(k) + s
+
+                @pl.when(dev // GROUP % LINE == z)
+                def _():
+                    body(dev, s, p, w * SEGS + k)
+
+            loop(SEGS - s, each)
+
+        one(a, 0)
+
+        @pl.when(b > a)
+        def _():
+            one(b, 1)
+
+    def to_line(start):
+        def each(n):
+            zz = near_first(n)
+            if start:
+                send(x_ref, line_buf.at[z], line_send.at[zz], line_recv.at[z], line(zz))
+            else:
+                sent(x_ref, line_send.at[zz], line(zz))
+
+        loop(LINE, each)
+
+    def spread(start):
+        def each(n):
+            zz = near_first(n)
+            src = line_buf.at[zz]
+            if start:
+                landed(src, line_recv.at[zz])
+
+            def body(dev, s, p, at):
+                if start:
+                    dst = x_col.at[pl.ds(p * SHARE, SHARE)]
+                    send(src, dst, spread_send.at[zz, at], gather_recv.at[1], dev)
+                else:
+                    sent(src, spread_send.at[zz, at], dev)
+
+            targets(zz, body)
+
+        loop(LINE, each)
 
     def to_relays(start):
         def body(s, w):
@@ -206,23 +254,8 @@
 
         return body
 
-    def to_columns(start):
-        def body(s, w):
-            dst = x_col.at[pl.ds((me - first_share(s)) * SHARE, SHARE)]
-
-            def each(n):
-                dev = tri(s + n) + s
-                if start:
-                    send(x_ref, dst, gather_send.at[w * SEGS + n], gather_recv.at[1], dev)
-                else:
-                    sent(x_ref, gather_send.at[w * SEGS + n], dev)
-
-            loop(SEGS - s, each)
-
-        return body
-
+    to_line(True)
     owned(to_relays(True))
-    owned(to_columns(True))
 
     for load in loads[1:]:
         load.wait()
@@ -252,6 +285,7 @@
 
         return body
 
+    spread(True)
     relayed(pass_on(True))
 
     def wait_rows(s, held, recv_sem):
@@ -316,14 +350,13 @@
     def col_parts(start):
         def each(p):
             owner = first_share(col) + p
+            dev = (owner // 64 * LINE + z) * GROUP + owner % GROUP
             if start:
-                second = place_of(owner, col)
-                send(
-                    chunk(1, p), arrived.at[second, KEYS + row], col_send.at[p],
-                    arrive_recv.at[second, KEYS + row], owner,
-                )
+                zz = owner // GROUP % LINE
+                at = place_of(owner, col) * SEGS + row
+                send(chunk(1, p), col_buf.at[zz, at], col_send.at[p], col_recv.at[zz, at], dev)
             else:
-                sent(chunk(1, p), col_send.at[p], owner)
+                sent(chunk(1, p), col_send.at[p], dev)
 
         loop(shares(col), each)
 
@@ -351,8 +384,9 @@
 
         col_parts(True)
 
+    to_line(False)
     owned(to_relays(False))
-    owned(to_columns(False))
+    spread(False)
     relayed(pass_on(False))
 
     def add_parts(start):
@@ -370,32 +404,41 @@
                 part_sum[key, turn] = lax.fori_loop(
                     0, count, each, jnp.zeros((ROWS, WIDTH), jnp.float32)
                 )
-                second = place_of(owner, s)
-                at = group - first_group(s)
-                send(
-                    src, arrived.at[second, at], sum_send.at[key, turn],
-                    arrive_recv.at[second, at], owner,
-                )
+                at = place_of(owner, s) * KEYS + group - first_group(s)
+                send(src, arrived.at[at], sum_send.at[key, turn], arrive_recv.at[at], owner)
             else:
                 sent(src, sum_send.at[key, turn], owner)
 
         return body
 
+    def add_cols(n):
+        zz = near_first(LINE - 1 - n)
+        col_sum[zz] = jnp.zeros((ROWS, WIDTH), jnp.float32)
+
+        def body(dev, s, p, at):
+            landed(col_buf.at[zz, at], col_recv.at[zz, at])
+            col_sum[zz] = col_sum[zz] + col_buf[zz, at]
+
+        targets(zz, body)
+        at = 2 * KEYS + z
+        send(col_sum.at[zz], arrived.at[at], back_send.at[zz], arrive_recv.at[at], line(zz))
+
     relayed(add_parts(True))
+    loop(LINE, add_cols)
+
+    def each(at, total):
+        landed(arrived.at[at], arrive_recv.at[at])
+        return total + arrived[at]
 
     def collect(w, s, total):
-        def each(at, total):
-            landed(arrived.at[w, at], arrive_recv.at[w, at])
-            return total + arrived[w, at]
-
-        total = lax.fori_loop(KEYS + s, KEYS + SEGS, each, total)
-        return lax.fori_loop(0, groups_of(s), each, total)
+        return lax.fori_loop(w * KEYS, w * KEYS + groups_of(s), each, total)
 
     def put(total):
         for t in range(SHARE):
             image_ref[t] = total[t * VEC:(t + 1) * VEC]
 
-    put(collect(0, seg_a, jnp.zeros((ROWS, WIDTH), jnp.float32)))
+    total = collect(0, seg_a, jnp.zeros((ROWS, WIDTH), jnp.float32))
+    put(lax.fori_loop(2 * KEYS, 2 * KEYS + LINE, each, total))
 
     @pl.when(two)
     def _():
@@ -414,11 +457,11 @@
     gram_own[0, :, VEC:2 * VEC] = both[VEC:]
 
     circles = (
-        (gram_a, z * 2 + core, lambda q: device(y, q // 2, x, q % 2)),
-        (gram_b, y * 4 + x, lambda q: device(q // 4, z, q % 4, core)),
+        (gram_a, z, LINE, line),
+        (gram_b, y * GROUP + residue, PLANE, plane),
     )
-    for n, (buf, rank, partner) in enumerate(circles):
-        for q in range(CIRCLE):
+    for n, (buf, rank, size, partner) in enumerate(circles):
+        for q in range(size):
             @pl.when(q != rank)
             def _():
                 pltpu.make_async_remote_copy(
@@ -438,8 +481,10 @@
             def _():
                 col_parts(False)
 
-        landed(buf.at[pl.ds(0, CIRCLE - 1)], gram_recv.at[n])
-        terms = [buf[q] for q in range(CIRCLE)]
+            loop(LINE, lambda zz: sent(col_sum.at[zz], back_send.at[zz], line(zz)))
+
+        landed(buf.at[pl.ds(0, size - 1)], gram_recv.at[n])
+        terms = [buf[q] for q in range(size)]
         while len(terms) > 1:
             terms = [a + b for a, b in zip(terms[::2], terms[1::2])]
         if n == 0:
@@ -447,8 +492,8 @@
         else:
             grams_ref[...] = terms[0] * (1.0 / (TILES * WIDTH))
 
-    for n, (_buf, rank, _partner) in enumerate(circles):
-        for q in range(CIRCLE):
+    for n, (_buf, rank, size, _partner) in enumerate(circles):
+        for q in range(size):
             @pl.when(q != rank)
             def _():
                 pltpu.make_async_copy(gram_own.at[n], gram_own.at[n], gram_send.at[n, q]).wait()
@@ -479,27 +524,34 @@
             pltpu.VMEM((WINDOW * SHARE, VEC, WIDTH), f32),
             pltpu.VMEM((WINDOW * SHARE, VEC, WIDTH), f32),
             pltpu.VMEM((KEYS, 2, SHARE, VEC, WIDTH), f32),
+            pltpu.VMEM((LINE, SHARE, VEC, WIDTH), f32),
+            pltpu.VMEM((LINE, 2 * SEGS, ROWS, WIDTH), f32),
+            pltpu.VMEM((LINE, ROWS, WIDTH), f32),
             pltpu.VMEM((SLOTS * VEC, WIDTH), f32),
             pltpu.VMEM((SLOTS * VEC, WIDTH), f32),
             pltpu.VMEM((2, PAD * VEC, WIDTH), f32),
             pltpu.VMEM((KEYS, 2, GROUP, ROWS, WIDTH), f32),
             pltpu.VMEM((KEYS, 2, ROWS, WIDTH), f32),
-            pltpu.VMEM((2, KEYS + SEGS, ROWS, WIDTH), f32),
+            pltpu.VMEM((2 * KEYS + LINE, ROWS, WIDTH), f32),
             pltpu.VMEM((2, VEC, WIDTH), f32),
-            pltpu.VMEM((CIRCLE, VEC, WIDTH), f32),
-            pltpu.VMEM((CIRCLE, VEC, WIDTH), f32),
+            pltpu.VMEM((LINE, VEC, WIDTH), f32),
+            pltpu.VMEM((PLANE, VEC, WIDTH), f32),
             dma((7,)),
             dma((2 * KEYS,)),
             dma((KEYS, 2)),
             dma((KEYS, 2, GROUP)),
-            dma((2 * SEGS,)),
+            dma((LINE,)),
+            dma((LINE,)),
+            dma((LINE, 2 * SEGS)),
             dma((2,)),
             dma((WINDOW,)),
             dma((KEYS, 2, GROUP)),
             dma((KEYS, 2)),
             dma((WINDOW,)),
-            dma((2, KEYS + SEGS)),
-            dma((2, CIRCLE)),
+            dma((LINE, 2 * SEGS)),
+            dma((LINE,)),
+            dma((2 * KEYS + LINE,)),
+            dma((2, PLANE)),
             dma((2,)),
         ],
         compiler_params=pltpu.CompilerParams(

time: 53.7 us -> 59.4 us (1.11)
  Pallas kernels: 51 us -> 56.5 us
    pallas_call x1, Pallas kernels: 51 us -> 56.5 us  [per_device(): pl.pallas_call(kernel, out_shape=(pltpu.VMEM((SHARE, VEC, WIDTH), f32), p...]
where the time goes in v4:
time: 59.4 us; the launch traced here: 59 us
  Pallas kernels  56.5 us (95%)
  between operations  1.29 us (2%)
  local copies, waits for them, and re-layouts  1.27 us (2%)
    pallas_call x1, Pallas kernels, per_device(): pl.pallas_call(kernel, out_shape=(pltpu.VMEM((SHARE, VEC, WIDTH), f32), p...  56.5 us

profile of v4, /device:TPU:1, one launch (start us, length us, event | category | flops | bytes accessed | tf_op | source)
XLA Modules:
  0.0 59.0 jit_solution(4326387285998896793)
XLA Ops:
  1.3 56.5 %shard_map.76 = (f32[4,8,128]{2,1,0:T(8,128)S(1)}, f32[8,128]{1,0:T(8,128)S(1)}) custom-call(f32[32,128,128]{2,1,0:T(8,128)} %tiles_ref.1, s32[32]{0:T(128)} %rows_hbm.1, s32[32]{0:T(128)} %cols_hbm.1, s32[1,32]{1,0:T(1,128)} %bitcast.2, s32[1,32]{1,0:T(1,128)} %bitcast.3, s32[1]{0:T(128)S(6)} %copy.10.count_hbm, f32[4,8,128]{2,1,0:T(8,128)} %x_hbm.1), custom_call_target="tpu_custom_call" | custom-call | tf_op jit(solution)/shard_map/pallas_call | solution.py:506
  57.8 0.6 %copy.9 = f32[4,8,128]{2,1,0:T(8,128)} copy(f32[4,8,128]{2,1,0:T(8,128)S(1)} %get-tuple-element.9) | data formatting | bytes 32768
  58.4 0.7 %fusion = (f32[8,8]{1,0:T(8,128)}, f32[8,8]{1,0:T(8,128)}) fusion(f32[8,128]{1,0:T(8,128)S(1)} %get-tuple-element.6), kind=kLoop, calls=%fused_computation | loop fusion | bytes 1024 | tf_op jit(solution)/shard_map/slice | solution.py:564

commit v5 on v4

--- a/solution.py
+++ b/solution.py
@@ -16,6 +16,8 @@
 WINDOW = 13
 PAD = 64
 BLOCKS = SEGS * (SEGS + 1) // 2
+DEVICES = 256
+LOW_SCALE, LOW_SHIFT = 2979, 6
 GROUP = 8
 LINE = 8
 PLANE = 32
@@ -25,38 +27,40 @@
 
 
 def seg_low(s):
-    return (s * TILES) // SEGS
+    return (s * LOW_SCALE) >> LOW_SHIFT
 
 
 def seg_of(t):
-    return ((t + 1) * SEGS - 1) // TILES
+    return ((t + 1) * SEGS - 1) >> 10
 
 
 def first_share(s):
-    return seg_low(s) // SHARE
+    return seg_low(s) >> 2
 
 
 def shares(s):
-    return (seg_low(s + 1) - 1) // SHARE - first_share(s) + 1
+    return ((seg_low(s + 1) - 1) >> 2) - first_share(s) + 1
 
 
 def tri(s):
-    return (s * (s + 1)) // 2
-
-
-def row_of(d):
-    row = 0
-    for m in range(1, SEGS):
-        row = row + jnp.where(d >= m * (m + 1) // 2, 1, 0)
+    return (s * (s + 1)) >> 1
+
+
+def row_of(d, low=0, high=DEVICES):
+    marks = [m * (m + 1) // 2 for m in range(1, SEGS)]
+    row = sum(m <= low for m in marks)
+    for m in marks:
+        if low < m < high:
+            row = row + (d >= m).astype(jnp.int32)
     return row
 
 
 def first_group(s):
-    return tri(s) // GROUP
+    return tri(s) >> 3
 
 
 def groups_of(s):
-    return (tri(s) + s - 1) // GROUP - first_group(s) + 1
+    return ((tri(s) + s - 1) >> 3) - first_group(s) + 1
 
 
 def split(a):
@@ -75,8 +79,8 @@
     part_send, part_recv, sum_send, col_send, col_recv, back_send, arrive_recv, gram_send, gram_recv,
 ):
     me = lax.axis_index("tri")
-    residue = me % GROUP
-    group = me // GROUP
+    residue = me & 7
+    group = me >> 3
     base = group * GROUP
     works = me < BLOCKS
     row = row_of(me)
@@ -119,13 +123,13 @@
     def relayed(body):
         def each(n):
             s = top + n
-            start = (residue - first_share(s) % GROUP + GROUP) % GROUP
+            start = (residue - first_share(s)) & 7
             for turn in range(2):
                 p = start + GROUP * turn
 
                 @pl.when(jnp.logical_and(p < shares(s), span(s)[1] > 0))
                 def _():
-                    body(s, p, s % KEYS, turn)
+                    body(s, p, s & 3, turn)
 
         loop(rows_here, each)
 
@@ -160,16 +164,16 @@
         def _():
             pl.semaphore_signal(barrier, inc=1, device_id=(dev,), device_id_type=MESH)
 
-    core, x, z, y = me % 2, residue // 2, group % LINE, me // 64
+    z, y = group & 7, me >> 6
 
     def line(zz):
         return (y * LINE + zz) * GROUP + residue
 
     def plane(q):
-        return (q // GROUP * LINE + z) * GROUP + q % GROUP
+        return ((q >> 3) * LINE + z) * GROUP + (q & 7)
 
     for dz in range(1, LINE):
-        greet(line((z + dz) % LINE))
+        greet(line((z + dz) & 7))
     for q in range(PLANE):
         greet(plane(q))
     relayed(lambda s, p, key, turn: greet(first_share(s) + p))
@@ -185,40 +189,36 @@
     loads[0].wait()
 
     def near_first(n):
-        return (z + jnp.where(n % 2 == 1, (n + 1) // 2, LINE - n // 2)) % LINE
+        return (z + jnp.where((n & 1) == 1, (n + 1) >> 1, LINE - (n >> 1))) & 7
 
     def targets(zz, body):
         owner = line(zz)
         a, b = seg_of(SHARE * owner), seg_of(SHARE * owner + SHARE - 1)
 
-        def one(s, w):
-            p = owner - first_share(s)
-
-            def each(n):
-                k = s + n
-                dev = tri(k) + s
-
-                @pl.when(dev // GROUP % LINE == z)
-                def _():
-                    body(dev, s, p, w * SEGS + k)
-
-            loop(SEGS - s, each)
-
-        one(a, 0)
+        def one(s):
+            for low, top_row, end_row in here:
+                def each(i, low=low, top_row=top_row):
+                    k = top_row + i
+                    dev = tri(k) + s
+
+                    @pl.when(jnp.logical_and(((dev - low) >> 3) == 0, s <= k))
+                    def _():
+                        body(dev, s, owner - first_share(s))
+
+                loop(end_row - top_row + 1, each)
+
+        one(a)
 
         @pl.when(b > a)
         def _():
-            one(b, 1)
-
-    def to_line(start):
-        def each(n):
-            zz = near_first(n)
-            if start:
-                send(x_ref, line_buf.at[z], line_send.at[zz], line_recv.at[z], line(zz))
-            else:
-                sent(x_ref, line_send.at[zz], line(zz))
-
-        loop(LINE, each)
+            one(b)
+
+    def rank_of(dev):
+        return ((dev >> 6) << 3) + (dev & 7)
+
+    def to_line(n):
+        zz = near_first(n)
+        send(x_ref, line_buf.at[z], line_send, line_recv.at[z], line(zz))
 
     def spread(start):
         def each(n):
@@ -227,12 +227,12 @@
             if start:
                 landed(src, line_recv.at[zz])
 
-            def body(dev, s, p, at):
+            def body(dev, s, p):
                 if start:
                     dst = x_col.at[pl.ds(p * SHARE, SHARE)]
-                    send(src, dst, spread_send.at[zz, at], gather_recv.at[1], dev)
+                    send(src, dst, spread_send, gather_recv.at[1], dev)
                 else:
-                    sent(src, spread_send.at[zz, at], dev)
+                    sent(src, spread_send, dev)
 
             targets(zz, body)
 
@@ -240,22 +240,29 @@
 
     def to_relays(start):
         def body(s, w):
-            turn = (me - first_share(s)) // GROUP
-            dst, sem = relay_buf.at[s % KEYS, turn], relay_recv.at[s % KEYS, turn]
+            turn = (me - first_share(s)) >> 3
+            dst, sem = relay_buf.at[s & 3, turn], relay_recv.at[s & 3, turn]
 
             def each(n):
                 dev = (first_group(s) + n) * GROUP + residue
                 if start:
-                    send(x_ref, dst, relay_send.at[w * KEYS + n], sem, dev)
+                    send(x_ref, dst, relay_send, sem, dev)
                 else:
-                    sent(x_ref, relay_send.at[w * KEYS + n], dev)
+                    sent(x_ref, relay_send, dev)
 
             loop(groups_of(s), each)
 
         return body
 
-    to_line(True)
+    loop(LINE, to_line)
     owned(to_relays(True))
+
+    here = []
+    for yy in range(4):
+        low = yy * 64 + z * GROUP
+        bounds = (yy * 64, yy * 64 + 64)
+        end = jnp.minimum(low + GROUP - 1, BLOCKS - 1)
+        here.append((low, row_of(low, *bounds), row_of(end, *bounds)))
 
     for load in loads[1:]:
         load.wait()
@@ -275,11 +282,10 @@
                 landed(src, relay_recv.at[key, turn])
 
             def each(dev):
-                sem = pass_send.at[key, turn, dev % GROUP]
                 if start:
-                    send(src, dst, sem, gather_recv.at[0], dev)
+                    send(src, dst, pass_send, gather_recv.at[0], dev)
                 else:
-                    sent(src, sem, dev)
+                    sent(src, pass_send, dev)
 
             members(s, each)
 
@@ -330,35 +336,34 @@
     def chunk(which, p):
         return contrib.at[which, pl.ds(pl.multiple_of(p * ROWS, ROWS), ROWS), :]
 
-    def row_parts(start):
-        def each(p):
-            dev = base + (first_share(row) + p) % GROUP
-            if start:
-                turn = p // GROUP
-                send(
-                    chunk(0, p), part_buf.at[row % KEYS, turn, residue], part_send.at[p],
-                    part_recv.at[row % KEYS, turn, residue], dev,
-                )
-            else:
-                sent(chunk(0, p), part_send.at[p], dev)
-
-        loop(shares(row), each)
+    def row_parts(p):
+        turn = p >> 3
+        send(
+            chunk(0, p), part_buf.at[turn, residue], part_send, part_recv.at[turn, residue],
+            base + ((first_share(row) + p) & 7),
+        )
+
+    def all_sent(which, s, same_y, sem):
+        n = shares(s)
+        for turn in range(2):
+            p = ((residue - first_share(s)) & 7) + GROUP * turn
+            mine = p < shares(s)
+            if same_y:
+                mine = jnp.logical_and(mine, ((first_share(s) + p) >> 6) == y)
+            n = n - mine.astype(jnp.int32)
+        for count in range(WINDOW - 3, WINDOW + 1):
+            @pl.when(n == count)
+            def _():
+                landed(contrib.at[which, pl.ds(0, count * ROWS), :], sem)
 
     def place_of(owner, s):
         return jnp.where(seg_of(SHARE * owner) == s, 0, 1)
 
-    def col_parts(start):
-        def each(p):
-            owner = first_share(col) + p
-            dev = (owner // 64 * LINE + z) * GROUP + owner % GROUP
-            if start:
-                zz = owner // GROUP % LINE
-                at = place_of(owner, col) * SEGS + row
-                send(chunk(1, p), col_buf.at[zz, at], col_send.at[p], col_recv.at[zz, at], dev)
-            else:
-                sent(chunk(1, p), col_send.at[p], dev)
-
-        loop(shares(col), each)
+    def col_parts(p):
+        owner = first_share(col) + p
+        at = rank_of(me) * 2 + (p >> 3)
+        dev = (((owner >> 6) << 3) + z) * GROUP + (owner & 7)
+        send(chunk(1, p), col_buf.at[at], col_send, col_recv.at[at], dev)
 
     @pl.when(works)
     def _():
@@ -368,7 +373,7 @@
 
         @pl.when(off_diagonal)
         def _():
-            row_parts(True)
+            loop(shares(row), row_parts)
             wait_rows(row, x_row, gather_recv.at[0])
             multiply(x_row, rows_ref, row_base, col_terms, 0, NN_DIMS)
 
@@ -382,9 +387,9 @@
         def _():
             contrib[1] = contrib[0] + contrib[1]
 
-        col_parts(True)
-
-    to_line(False)
+        loop(shares(col), col_parts)
+
+    landed(line_buf.at[pl.ds(0, LINE - 1)], line_send)
     owned(to_relays(False))
     spread(False)
     relayed(pass_on(False))
@@ -397,17 +402,17 @@
                 low, count = span(s)
 
                 def each(i, total):
-                    rank = (low + i) % GROUP
-                    landed(part_buf.at[key, turn, rank], part_recv.at[key, turn, rank])
-                    return total + part_buf[key, turn, rank]
+                    rank = (low + i) & 7
+                    landed(part_buf.at[turn, rank], part_recv.at[turn, rank])
+                    return total + part_buf[turn, rank]
 
                 part_sum[key, turn] = lax.fori_loop(
                     0, count, each, jnp.zeros((ROWS, WIDTH), jnp.float32)
                 )
                 at = place_of(owner, s) * KEYS + group - first_group(s)
-                send(src, arrived.at[at], sum_send.at[key, turn], arrive_recv.at[at], owner)
+                send(src, arrived.at[at], sum_send, arrive_recv.at[at], owner)
             else:
-                sent(src, sum_send.at[key, turn], owner)
+                sent(src, sum_send, owner)
 
         return body
 
@@ -415,13 +420,14 @@
         zz = near_first(LINE - 1 - n)
         col_sum[zz] = jnp.zeros((ROWS, WIDTH), jnp.float32)
 
-        def body(dev, s, p, at):
-            landed(col_buf.at[zz, at], col_recv.at[zz, at])
-            col_sum[zz] = col_sum[zz] + col_buf[zz, at]
+        def body(dev, s, p):
+            at = rank_of(dev) * 2 + (p >> 3)
+            landed(col_buf.at[at], col_recv.at[at])
+            col_sum[zz] = col_sum[zz] + col_buf[at]
 
         targets(zz, body)
         at = 2 * KEYS + z
-        send(col_sum.at[zz], arrived.at[at], back_send.at[zz], arrive_recv.at[at], line(zz))
+        send(col_sum.at[zz], arrived.at[at], back_send, arrive_recv.at[at], line(zz))
 
     relayed(add_parts(True))
     loop(LINE, add_cols)
@@ -465,7 +471,7 @@
             @pl.when(q != rank)
             def _():
                 pltpu.make_async_remote_copy(
-                    src_ref=gram_own.at[n], dst_ref=buf.at[rank], send_sem=gram_send.at[n, q],
+                    src_ref=gram_own.at[n], dst_ref=buf.at[rank], send_sem=gram_send.at[n],
                     recv_sem=gram_recv.at[n], device_id=(partner(q),), device_id_type=MESH,
                 ).start()
 
@@ -475,13 +481,13 @@
 
             @pl.when(off_diagonal)
             def _():
-                row_parts(False)
+                all_sent(0, row, False, part_send)
 
             @pl.when(works)
             def _():
-                col_parts(False)
-
-            loop(LINE, lambda zz: sent(col_sum.at[zz], back_send.at[zz], line(zz)))
+                all_sent(1, col, True, col_send)
+
+            landed(col_sum.at[pl.ds(0, LINE - 1)], back_send)
 
         landed(buf.at[pl.ds(0, size - 1)], gram_recv.at[n])
         terms = [buf[q] for q in range(size)]
@@ -492,11 +498,8 @@
         else:
             grams_ref[...] = terms[0] * (1.0 / (TILES * WIDTH))
 
-    for n, (_buf, rank, size, _partner) in enumerate(circles):
-        for q in range(size):
-            @pl.when(q != rank)
-            def _():
-                pltpu.make_async_copy(gram_own.at[n], gram_own.at[n], gram_send.at[n, q]).wait()
+    for n, (buf, _rank, size, _partner) in enumerate(circles):
+        landed(buf.at[pl.ds(0, size - 1)], gram_send.at[n])
 
 
 def per_device(tiles, tile_rows, tile_cols, counts, block_vectors):
@@ -525,33 +528,33 @@
             pltpu.VMEM((WINDOW * SHARE, VEC, WIDTH), f32),
             pltpu.VMEM((KEYS, 2, SHARE, VEC, WIDTH), f32),
             pltpu.VMEM((LINE, SHARE, VEC, WIDTH), f32),
-            pltpu.VMEM((LINE, 2 * SEGS, ROWS, WIDTH), f32),
+            pltpu.VMEM((2 * PLANE, ROWS, WIDTH), f32),
             pltpu.VMEM((LINE, ROWS, WIDTH), f32),
             pltpu.VMEM((SLOTS * VEC, WIDTH), f32),
             pltpu.VMEM((SLOTS * VEC, WIDTH), f32),
             pltpu.VMEM((2, PAD * VEC, WIDTH), f32),
-            pltpu.VMEM((KEYS, 2, GROUP, ROWS, WIDTH), f32),
+            pltpu.VMEM((2, GROUP, ROWS, WIDTH), f32),
             pltpu.VMEM((KEYS, 2, ROWS, WIDTH), f32),
             pltpu.VMEM((2 * KEYS + LINE, ROWS, WIDTH), f32),
             pltpu.VMEM((2, VEC, WIDTH), f32),
             pltpu.VMEM((LINE, VEC, WIDTH), f32),
             pltpu.VMEM((PLANE, VEC, WIDTH), f32),
             dma((7,)),
-            dma((2 * KEYS,)),
+            dma,
             dma((KEYS, 2)),
-            dma((KEYS, 2, GROUP)),
+            dma,
+            dma,
             dma((LINE,)),
-            dma((LINE,)),
-            dma((LINE, 2 * SEGS)),
+            dma,
             dma((2,)),
-            dma((WINDOW,)),
-            dma((KEYS, 2, GROUP)),
-            dma((KEYS, 2)),
-            dma((WINDOW,)),
-            dma((LINE, 2 * SEGS)),
-            dma((LINE,)),
+            dma,
+            dma((2, GROUP)),
+            dma,
+            dma,
+            dma((2 * PLANE,)),
+            dma,
             dma((2 * KEYS + LINE,)),
-            dma((2, PLANE)),
+            dma((2,)),
             dma((2,)),
         ],
         compiler_params=pltpu.CompilerParams(

time: 59.4 us -> 49.6 us (0.84)
  Pallas kernels: 56.5 us -> 47 us
    pallas_call x1, Pallas kernels: 56.5 us -> 47 us  [per_device(): pl.pallas_call(kernel, out_shape=(pltpu.VMEM((SHARE, VEC, WIDTH), f32), p...]
where the time goes in v5:
time: 49.6 us; the launch traced here: 49.5 us
  Pallas kernels  47 us (95%)
  between operations  1.29 us (3%)
  local copies, waits for them, and re-layouts  1.27 us (3%)
    pallas_call x1, Pallas kernels, per_device(): pl.pallas_call(kernel, out_shape=(pltpu.VMEM((SHARE, VEC, WIDTH), f32), p...  47 us

profile of v5, /device:TPU:1, one launch (start us, length us, event | category | flops | bytes accessed | tf_op | source)
XLA Modules:
  0.0 49.5 jit_solution(13155221653792687637)
XLA Ops:
  1.3 47.0 %shard_map.76 = (f32[4,8,128]{2,1,0:T(8,128)S(1)}, f32[8,128]{1,0:T(8,128)S(1)}) custom-call(f32[32,128,128]{2,1,0:T(8,128)} %tiles_ref.1, s32[32]{0:T(128)} %rows_hbm.1, s32[32]{0:T(128)} %cols_hbm.1, s32[1,32]{1,0:T(1,128)} %bitcast.2, s32[1,32]{1,0:T(1,128)} %bitcast.3, s32[1]{0:T(128)S(6)} %copy.10.count_hbm, f32[4,8,128]{2,1,0:T(8,128)} %x_hbm.1), custom_call_target="tpu_custom_call" | custom-call | tf_op jit(solution)/shard_map/pallas_call | solution.py:509
  48.3 0.6 %copy.9 = f32[4,8,128]{2,1,0:T(8,128)} copy(f32[4,8,128]{2,1,0:T(8,128)S(1)} %get-tuple-element.9) | data formatting | bytes 32768
  48.9 0.7 %fusion = (f32[8,8]{1,0:T(8,128)}, f32[8,8]{1,0:T(8,128)}) fusion(f32[8,128]{1,0:T(8,128)S(1)} %get-tuple-element.6), kind=kLoop, calls=%fused_computation | loop fusion | bytes 1024 | tf_op jit(solution)/shard_map/slice | solution.py:567

commit v6 on v5

--- a/solution.py
+++ b/solution.py
@@ -21,6 +21,7 @@
 GROUP = 8
 LINE = 8
 PLANE = 32
+ROWS_AT = (4, 2, 2, 2)
 KEYS = 4
 NT_DIMS = (((1,), (1,)), ((), ()))
 NN_DIMS = (((1,), (0,)), ((), ()))
@@ -73,10 +74,10 @@
     tiles_ref, rows_hbm, cols_hbm, rows_hbm2, cols_hbm2, count_hbm, x_hbm,
     image_ref, grams_ref,
     tile_buf, hi_buf, lo_buf, x_ref, rows_ref, cols_ref, rows_vec, cols_vec, count_ref,
-    x_row, x_col, relay_buf, line_buf, col_buf, col_sum, row_terms, col_terms, contrib, part_buf, part_sum, arrived,
+    x_row, x_col, relay_buf, line_buf, row_terms, col_terms, contrib, part_buf, part_sum, arrived,
     gram_own, gram_a, gram_b,
     in_sem, relay_send, relay_recv, pass_send, line_send, line_recv, spread_send, gather_recv,
-    part_send, part_recv, sum_send, col_send, col_recv, back_send, arrive_recv, gram_send, gram_recv,
+    part_send, part_recv, sum_send, col_send, arrive_recv, gram_send, gram_recv,
 ):
     me = lax.axis_index("tri")
     residue = me & 7
@@ -138,16 +139,16 @@
         loop(count, lambda i: body(low + i))
 
     def send(src, dst, send_sem, recv_sem, dev):
-        @pl.when(dev != me)
-        def _():
+        def remote():
             pltpu.make_async_remote_copy(
                 src_ref=src, dst_ref=dst, send_sem=send_sem, recv_sem=recv_sem,
                 device_id=(dev,), device_id_type=MESH,
             ).start()
 
-        @pl.when(dev == me)
-        def _():
+        def local():
             pltpu.make_async_copy(src, dst, recv_sem).start()
+
+        lax.cond(dev != me, remote, local)
 
     def sent(src, send_sem, dev):
         @pl.when(dev != me)
@@ -166,6 +167,9 @@
 
     z, y = group & 7, me >> 6
 
+    def rank_of(dev):
+        return ((dev >> 6) << 3) + (dev & 7)
+
     def line(zz):
         return (y * LINE + zz) * GROUP + residue
 
@@ -173,9 +177,11 @@
         return ((q >> 3) * LINE + z) * GROUP + (q & 7)
 
     for dz in range(1, LINE):
-        greet(line((z + dz) & 7))
-    for q in range(PLANE):
-        greet(plane(q))
+        pl.semaphore_signal(barrier, inc=1, device_id=(line((z + dz) & 7),), device_id_type=MESH)
+    for m in range(1, PLANE):
+        pl.semaphore_signal(
+            barrier, inc=1, device_id=(plane(rank_of(me) ^ m),), device_id_type=MESH
+        )
     relayed(lambda s, p, key, turn: greet(first_share(s) + p))
 
     for load in loads[1:]:
@@ -195,29 +201,20 @@
         owner = line(zz)
         a, b = seg_of(SHARE * owner), seg_of(SHARE * owner + SHARE - 1)
 
-        def one(s):
-            for low, top_row, end_row in here:
-                def each(i, low=low, top_row=top_row):
-                    k = top_row + i
-                    dev = tri(k) + s
-
-                    @pl.when(jnp.logical_and(((dev - low) >> 3) == 0, s <= k))
-                    def _():
-                        body(dev, s, owner - first_share(s))
-
-                loop(end_row - top_row + 1, each)
-
-        one(a)
-
-        @pl.when(b > a)
-        def _():
-            one(b)
-
-    def rank_of(dev):
-        return ((dev >> 6) << 3) + (dev & 7)
+        def one(w):
+            s = a + w
+            p = owner - first_share(s)
+            for k, first, low in here:
+                dev = first + s
+
+                @pl.when(jnp.logical_and(((dev - low) >> 3) == 0, s <= k))
+                def _(dev=dev):
+                    body(dev, s, p)
+
+        loop(1 + (b > a).astype(jnp.int32), one)
 
     def to_line(n):
-        zz = near_first(n)
+        zz = near_first(LINE - 1 - n)
         send(x_ref, line_buf.at[z], line_send, line_recv.at[z], line(zz))
 
     def spread(start):
@@ -258,11 +255,11 @@
     owned(to_relays(True))
 
     here = []
-    for yy in range(4):
+    for yy in (2, 1, 3, 0):
         low = yy * 64 + z * GROUP
-        bounds = (yy * 64, yy * 64 + 64)
-        end = jnp.minimum(low + GROUP - 1, BLOCKS - 1)
-        here.append((low, row_of(low, *bounds), row_of(end, *bounds)))
+        first_row = row_of(low, yy * 64, yy * 64 + 64)
+        for k in [first_row + i for i in range(ROWS_AT[yy])]:
+            here.append((k, jnp.where(k < SEGS, tri(k), 2 * DEVICES), low))
 
     for load in loads[1:]:
         load.wait()
@@ -343,14 +340,7 @@
             base + ((first_share(row) + p) & 7),
         )
 
-    def all_sent(which, s, same_y, sem):
-        n = shares(s)
-        for turn in range(2):
-            p = ((residue - first_share(s)) & 7) + GROUP * turn
-            mine = p < shares(s)
-            if same_y:
-                mine = jnp.logical_and(mine, ((first_share(s) + p) >> 6) == y)
-            n = n - mine.astype(jnp.int32)
+    def all_sent(which, n, sem):
         for count in range(WINDOW - 3, WINDOW + 1):
             @pl.when(n == count)
             def _():
@@ -359,11 +349,13 @@
     def place_of(owner, s):
         return jnp.where(seg_of(SHARE * owner) == s, 0, 1)
 
+    def slot_of(owner, s):
+        return place_of(owner, s) * (KEYS + SEGS)
+
     def col_parts(p):
         owner = first_share(col) + p
-        at = rank_of(me) * 2 + (p >> 3)
-        dev = (((owner >> 6) << 3) + z) * GROUP + (owner & 7)
-        send(chunk(1, p), col_buf.at[at], col_send, col_recv.at[at], dev)
+        at = slot_of(owner, col) + KEYS + row
+        send(chunk(1, p), arrived.at[at], col_send, arrive_recv.at[at], owner)
 
     @pl.when(works)
     def _():
@@ -409,42 +401,29 @@
                 part_sum[key, turn] = lax.fori_loop(
                     0, count, each, jnp.zeros((ROWS, WIDTH), jnp.float32)
                 )
-                at = place_of(owner, s) * KEYS + group - first_group(s)
+                at = slot_of(owner, s) + group - first_group(s)
                 send(src, arrived.at[at], sum_send, arrive_recv.at[at], owner)
             else:
                 sent(src, sum_send, owner)
 
         return body
 
-    def add_cols(n):
-        zz = near_first(LINE - 1 - n)
-        col_sum[zz] = jnp.zeros((ROWS, WIDTH), jnp.float32)
-
-        def body(dev, s, p):
-            at = rank_of(dev) * 2 + (p >> 3)
-            landed(col_buf.at[at], col_recv.at[at])
-            col_sum[zz] = col_sum[zz] + col_buf[at]
-
-        targets(zz, body)
-        at = 2 * KEYS + z
-        send(col_sum.at[zz], arrived.at[at], back_send, arrive_recv.at[at], line(zz))
-
     relayed(add_parts(True))
-    loop(LINE, add_cols)
 
     def each(at, total):
         landed(arrived.at[at], arrive_recv.at[at])
         return total + arrived[at]
 
     def collect(w, s, total):
-        return lax.fori_loop(w * KEYS, w * KEYS + groups_of(s), each, total)
+        start = w * (KEYS + SEGS)
+        total = lax.fori_loop(start + KEYS + s, start + KEYS + SEGS, each, total)
+        return lax.fori_loop(start, start + groups_of(s), each, total)
 
     def put(total):
         for t in range(SHARE):
             image_ref[t] = total[t * VEC:(t + 1) * VEC]
 
-    total = collect(0, seg_a, jnp.zeros((ROWS, WIDTH), jnp.float32))
-    put(lax.fori_loop(2 * KEYS, 2 * KEYS + LINE, each, total))
+    put(collect(0, seg_a, jnp.zeros((ROWS, WIDTH), jnp.float32)))
 
     @pl.when(two)
     def _():
@@ -462,18 +441,20 @@
     gram_own[0, :, 0:VEC] = both[:VEC]
     gram_own[0, :, VEC:2 * VEC] = both[VEC:]
 
+    def hops(m):
+        return [0, 1, 2, 1][m >> 3] + [0, 1, 2, 1][(m >> 1) & 3]
+
+    rank = rank_of(me)
     circles = (
-        (gram_a, z, LINE, line),
-        (gram_b, y * GROUP + residue, PLANE, plane),
+        (gram_a, z, LINE, [line((z + dz) & 7) for dz in (4, 3, 5, 2, 6, 1, 7)]),
+        (gram_b, rank, PLANE, [plane(rank ^ m) for m in sorted(range(1, PLANE), key=hops, reverse=True)]),
     )
-    for n, (buf, rank, size, partner) in enumerate(circles):
-        for q in range(size):
-            @pl.when(q != rank)
-            def _():
-                pltpu.make_async_remote_copy(
-                    src_ref=gram_own.at[n], dst_ref=buf.at[rank], send_sem=gram_send.at[n],
-                    recv_sem=gram_recv.at[n], device_id=(partner(q),), device_id_type=MESH,
-                ).start()
+    for n, (buf, rank, size, partners) in enumerate(circles):
+        for dev in partners:
+            pltpu.make_async_remote_copy(
+                src_ref=gram_own.at[n], dst_ref=buf.at[rank], send_sem=gram_send.at[n],
+                recv_sem=gram_recv.at[n], device_id=(dev,), device_id_type=MESH,
+            ).start()
 
         buf[rank] = gram_own[n]
         if n == 0:
@@ -481,13 +462,15 @@
 
             @pl.when(off_diagonal)
             def _():
-                all_sent(0, row, False, part_send)
+                p = (residue - first_share(row)) & 7
+                n_sent = shares(row) - 1 - (p + GROUP < shares(row)).astype(jnp.int32)
+                all_sent(0, n_sent, part_send)
 
             @pl.when(works)
             def _():
-                all_sent(1, col, True, col_send)
-
-            landed(col_sum.at[pl.ds(0, LINE - 1)], back_send)
+                p = me - first_share(col)
+                mine = jnp.logical_and(p >= 0, p < shares(col)).astype(jnp.int32)
+                all_sent(1, shares(col) - mine, col_send)
 
         landed(buf.at[pl.ds(0, size - 1)], gram_recv.at[n])
         terms = [buf[q] for q in range(size)]
@@ -498,7 +481,7 @@
         else:
             grams_ref[...] = terms[0] * (1.0 / (TILES * WIDTH))
 
-    for n, (buf, _rank, size, _partner) in enumerate(circles):
+    for n, (buf, _rank, size, _partners) in enumerate(circles):
         landed(buf.at[pl.ds(0, size - 1)], gram_send.at[n])
 
 
@@ -528,14 +511,12 @@
             pltpu.VMEM((WINDOW * SHARE, VEC, WIDTH), f32),
             pltpu.VMEM((KEYS, 2, SHARE, VEC, WIDTH), f32),
             pltpu.VMEM((LINE, SHARE, VEC, WIDTH), f32),
-            pltpu.VMEM((2 * PLANE, ROWS, WIDTH), f32),
-            pltpu.VMEM((LINE, ROWS, WIDTH), f32),
             pltpu.VMEM((SLOTS * VEC, WIDTH), f32),
             pltpu.VMEM((SLOTS * VEC, WIDTH), f32),
             pltpu.VMEM((2, PAD * VEC, WIDTH), f32),
             pltpu.VMEM((2, GROUP, ROWS, WIDTH), f32),
             pltpu.VMEM((KEYS, 2, ROWS, WIDTH), f32),
-            pltpu.VMEM((2 * KEYS + LINE, ROWS, WIDTH), f32),
+            pltpu.VMEM((2 * (KEYS + SEGS), ROWS, WIDTH), f32),
             pltpu.VMEM((2, VEC, WIDTH), f32),
             pltpu.VMEM((LINE, VEC, WIDTH), f32),
             pltpu.VMEM((PLANE, VEC, WIDTH), f32),
@@ -551,9 +532,7 @@
             dma((2, GROUP)),
             dma,
             dma,
-            dma((2 * PLANE,)),
-            dma,
-            dma((2 * KEYS + LINE,)),
+            dma((2 * (KEYS + SEGS),)),
             dma((2,)),
             dma((2,)),
         ],

time: 49.6 us -> 50.9 us (1.026)
  Pallas kernels: 47 us -> 48.2 us
    pallas_call x1, Pallas kernels: 47 us -> 48.2 us  [per_device(): pl.pallas_call(kernel, out_shape=(pltpu.VMEM((SHARE, VEC, WIDTH), f32), p...]
where the time goes in v6:
time: 50.9 us; the launch traced here: 50.8 us
  Pallas kernels  48.2 us (95%)
  between operations  1.29 us (3%)
  local copies, waits for them, and re-layouts  1.27 us (2%)
    pallas_call x1, Pallas kernels, per_device(): pl.pallas_call(kernel, out_shape=(pltpu.VMEM((SHARE, VEC, WIDTH), f32), p...  48.2 us

profile of v6, /device:TPU:1, one launch (start us, length us, event | category | flops | bytes accessed | tf_op | source)
XLA Modules:
  0.0 50.8 jit_solution(196626655140599152)
XLA Ops:
  1.3 48.2 %shard_map.76 = (f32[4,8,128]{2,1,0:T(8,128)S(1)}, f32[8,128]{1,0:T(8,128)S(1)}) custom-call(f32[32,128,128]{2,1,0:T(8,128)} %tiles_ref.1, s32[32]{0:T(128)} %rows_hbm.1, s32[32]{0:T(128)} %cols_hbm.1, s32[1,32]{1,0:T(1,128)} %bitcast.2, s32[1,32]{1,0:T(1,128)} %bitcast.3, s32[1]{0:T(128)S(6)} %copy.10.count_hbm, f32[4,8,128]{2,1,0:T(8,128)} %x_hbm.1), custom_call_target="tpu_custom_call" | custom-call | tf_op jit(solution)/shard_map/pallas_call | solution.py:492
  49.5 0.6 %copy.9 = f32[4,8,128]{2,1,0:T(8,128)} copy(f32[4,8,128]{2,1,0:T(8,128)S(1)} %get-tuple-element.9) | data formatting | bytes 32768
  50.1 0.7 %fusion = (f32[8,8]{1,0:T(8,128)}, f32[8,8]{1,0:T(8,128)}) fusion(f32[8,128]{1,0:T(8,128)S(1)} %get-tuple-element.6), kind=kLoop, calls=%fused_computation | loop fusion | bytes 1024 | tf_op jit(solution)/shard_map/slice | solution.py:546

commit v7 on v6

--- a/solution.py
+++ b/solution.py
@@ -21,7 +21,6 @@
 GROUP = 8
 LINE = 8
 PLANE = 32
-ROWS_AT = (4, 2, 2, 2)
 KEYS = 4
 NT_DIMS = (((1,), (1,)), ((), ()))
 NN_DIMS = (((1,), (0,)), ((), ()))
@@ -74,9 +73,9 @@
     tiles_ref, rows_hbm, cols_hbm, rows_hbm2, cols_hbm2, count_hbm, x_hbm,
     image_ref, grams_ref,
     tile_buf, hi_buf, lo_buf, x_ref, rows_ref, cols_ref, rows_vec, cols_vec, count_ref,
-    x_row, x_col, relay_buf, line_buf, row_terms, col_terms, contrib, part_buf, part_sum, arrived,
+    x_row, x_col, relay_buf, row_terms, col_terms, contrib, part_buf, part_sum, arrived,
     gram_own, gram_a, gram_b,
-    in_sem, relay_send, relay_recv, pass_send, line_send, line_recv, spread_send, gather_recv,
+    in_sem, relay_send, relay_recv, pass_send, direct_send, gather_recv,
     part_send, part_recv, sum_send, col_send, arrive_recv, gram_send, gram_recv,
 ):
     me = lax.axis_index("tri")
@@ -176,6 +175,10 @@
     def plane(q):
         return ((q >> 3) * LINE + z) * GROUP + (q & 7)
 
+    @pl.when(works)
+    def _():
+        loop(shares(col), lambda p: greet(first_share(col) + p))
+
     for dz in range(1, LINE):
         pl.semaphore_signal(barrier, inc=1, device_id=(line((z + dz) & 7),), device_id_type=MESH)
     for m in range(1, PLANE):
@@ -189,51 +192,26 @@
 
     def greeters(s):
         mine = jnp.logical_and(group >= first_group(s), group < first_group(s) + groups_of(s))
-        return groups_of(s) - jnp.where(mine, 1, 0)
+        n = groups_of(s) - jnp.where(mine, 1, 0)
+        return n + SEGS - s - jnp.logical_and(works, col == s).astype(jnp.int32)
 
     pl.semaphore_wait(barrier, LINE + PLANE - 2 + greeters(seg_a) + jnp.where(two, greeters(seg_b), 0))
     loads[0].wait()
 
-    def near_first(n):
-        return (z + jnp.where((n & 1) == 1, (n + 1) >> 1, LINE - (n >> 1))) & 7
-
-    def targets(zz, body):
-        owner = line(zz)
-        a, b = seg_of(SHARE * owner), seg_of(SHARE * owner + SHARE - 1)
-
-        def one(w):
-            s = a + w
-            p = owner - first_share(s)
-            for k, first, low in here:
-                dev = first + s
-
-                @pl.when(jnp.logical_and(((dev - low) >> 3) == 0, s <= k))
-                def _(dev=dev):
-                    body(dev, s, p)
-
-        loop(1 + (b > a).astype(jnp.int32), one)
-
-    def to_line(n):
-        zz = near_first(LINE - 1 - n)
-        send(x_ref, line_buf.at[z], line_send, line_recv.at[z], line(zz))
-
-    def spread(start):
-        def each(n):
-            zz = near_first(n)
-            src = line_buf.at[zz]
-            if start:
-                landed(src, line_recv.at[zz])
-
-            def body(dev, s, p):
+    def to_columns(start):
+        def body(s, w):
+            dst = x_col.at[pl.ds((me - first_share(s)) * SHARE, SHARE)]
+
+            def each(n):
+                dev = tri(s + n) + s
                 if start:
-                    dst = x_col.at[pl.ds(p * SHARE, SHARE)]
-                    send(src, dst, spread_send, gather_recv.at[1], dev)
+                    send(x_ref, dst, direct_send, gather_recv.at[1], dev)
                 else:
-                    sent(src, spread_send, dev)
-
-            targets(zz, body)
-
-        loop(LINE, each)
+                    sent(x_ref, direct_send, dev)
+
+            loop(SEGS - s, each)
+
+        return body
 
     def to_relays(start):
         def body(s, w):
@@ -251,15 +229,8 @@
 
         return body
 
-    loop(LINE, to_line)
     owned(to_relays(True))
-
-    here = []
-    for yy in (2, 1, 3, 0):
-        low = yy * 64 + z * GROUP
-        first_row = row_of(low, yy * 64, yy * 64 + 64)
-        for k in [first_row + i for i in range(ROWS_AT[yy])]:
-            here.append((k, jnp.where(k < SEGS, tri(k), 2 * DEVICES), low))
+    owned(to_columns(True))
 
     for load in loads[1:]:
         load.wait()
@@ -288,7 +259,6 @@
 
         return body
 
-    spread(True)
     relayed(pass_on(True))
 
     def wait_rows(s, held, recv_sem):
@@ -381,9 +351,8 @@
 
         loop(shares(col), col_parts)
 
-    landed(line_buf.at[pl.ds(0, LINE - 1)], line_send)
     owned(to_relays(False))
-    spread(False)
+    owned(to_columns(False))
     relayed(pass_on(False))
 
     def add_parts(start):
@@ -510,7 +479,6 @@
             pltpu.VMEM((WINDOW * SHARE, VEC, WIDTH), f32),
             pltpu.VMEM((WINDOW * SHARE, VEC, WIDTH), f32),
             pltpu.VMEM((KEYS, 2, SHARE, VEC, WIDTH), f32),
-            pltpu.VMEM((LINE, SHARE, VEC, WIDTH), f32),
             pltpu.VMEM((SLOTS * VEC, WIDTH), f32),
             pltpu.VMEM((SLOTS * VEC, WIDTH), f32),
             pltpu.VMEM((2, PAD * VEC, WIDTH), f32),
@@ -524,8 +492,6 @@
             dma,
             dma((KEYS, 2)),
             dma,
-            dma,
-            dma((LINE,)),
             dma,
             dma((2,)),
             dma,

time: 50.9 us -> 52.7 us (1.035)
  Pallas kernels: 48.2 us -> 50.1 us
    pallas_call x1, Pallas kernels: 48.2 us -> 50.1 us  [per_device(): pl.pallas_call(kernel, out_shape=(pltpu.VMEM((SHARE, VEC, WIDTH), f32), p...]
where the time goes in v7:
time: 52.7 us; the launch traced here: 52.6 us
  Pallas kernels  50.1 us (95%)
  between operations  1.29 us (2%)
  local copies, waits for them, and re-layouts  1.27 us (2%)
    pallas_call x1, Pallas kernels, per_device(): pl.pallas_call(kernel, out_shape=(pltpu.VMEM((SHARE, VEC, WIDTH), f32), p...  50.1 us

profile of v7, /device:TPU:1, one launch (start us, length us, event | category | flops | bytes accessed | tf_op | source)
XLA Modules:
  0.0 52.6 jit_solution(5085827624471621676)
XLA Ops:
  1.3 50.1 %shard_map.76 = (f32[4,8,128]{2,1,0:T(8,128)S(1)}, f32[8,128]{1,0:T(8,128)S(1)}) custom-call(f32[32,128,128]{2,1,0:T(8,128)} %tiles_ref.1, s32[32]{0:T(128)} %rows_hbm.1, s32[32]{0:T(128)} %cols_hbm.1, s32[1,32]{1,0:T(1,128)} %bitcast.2, s32[1,32]{1,0:T(1,128)} %bitcast.3, s32[1]{0:T(128)S(6)} %copy.10.count_hbm, f32[4,8,128]{2,1,0:T(8,128)} %x_hbm.1), custom_call_target="tpu_custom_call" | custom-call | tf_op jit(solution)/shard_map/pallas_call | solution.py:461
  51.3 0.6 %copy.9 = f32[4,8,128]{2,1,0:T(8,128)} copy(f32[4,8,128]{2,1,0:T(8,128)S(1)} %get-tuple-element.9) | data formatting | bytes 32768
  52.0 0.7 %fusion = (f32[8,8]{1,0:T(8,128)}, f32[8,8]{1,0:T(8,128)}) fusion(f32[8,128]{1,0:T(8,128)S(1)} %get-tuple-element.6), kind=kLoop, calls=%fused_computation | loop fusion | bytes 1024 | tf_op jit(solution)/shard_map/slice | solution.py:512

commit v8 on v6

--- a/solution.py
+++ b/solution.py
@@ -74,10 +74,10 @@
     tiles_ref, rows_hbm, cols_hbm, rows_hbm2, cols_hbm2, count_hbm, x_hbm,
     image_ref, grams_ref,
     tile_buf, hi_buf, lo_buf, x_ref, rows_ref, cols_ref, rows_vec, cols_vec, count_ref,
-    x_row, x_col, relay_buf, line_buf, row_terms, col_terms, contrib, part_buf, part_sum, arrived,
-    gram_own, gram_a, gram_b,
+    x_row, x_col, relay_buf, line_buf, col_buf, col_sum, row_terms, col_terms, contrib, part_buf, part_sum, arrived,
+    gram_tile, gram_own, gram_a, gram_b,
     in_sem, relay_send, relay_recv, pass_send, line_send, line_recv, spread_send, gather_recv,
-    part_send, part_recv, sum_send, col_send, arrive_recv, gram_send, gram_recv,
+    part_send, part_recv, sum_send, col_send, col_recv, back_send, arrive_recv, gram_send, gram_recv,
 ):
     me = lax.axis_index("tri")
     residue = me & 7
@@ -101,8 +101,6 @@
             (rows_hbm2, rows_vec), (cols_hbm2, cols_vec), (count_hbm, count_ref),
         ))
     ]
-    loads[0].start()
-
     def loop(n, body):
         def step(i, _):
             body(i)
@@ -176,23 +174,22 @@
     def plane(q):
         return ((q >> 3) * LINE + z) * GROUP + (q & 7)
 
-    for dz in range(1, LINE):
+    relayed(lambda s, p, key, turn: greet(first_share(s) + p))
+    for dz in (4, 3, 5, 2, 6, 1, 7):
         pl.semaphore_signal(barrier, inc=1, device_id=(line((z + dz) & 7),), device_id_type=MESH)
-    for m in range(1, PLANE):
+    def hops(m):
+        return [0, 1, 2, 1][m >> 3] + [0, 1, 2, 1][(m >> 1) & 3]
+
+    far_first = sorted(range(1, PLANE), key=hops, reverse=True)
+    for m in far_first:
         pl.semaphore_signal(
             barrier, inc=1, device_id=(plane(rank_of(me) ^ m),), device_id_type=MESH
         )
-    relayed(lambda s, p, key, turn: greet(first_share(s) + p))
-
-    for load in loads[1:]:
-        load.start()
-
     def greeters(s):
         mine = jnp.logical_and(group >= first_group(s), group < first_group(s) + groups_of(s))
         return groups_of(s) - jnp.where(mine, 1, 0)
 
     pl.semaphore_wait(barrier, LINE + PLANE - 2 + greeters(seg_a) + jnp.where(two, greeters(seg_b), 0))
-    loads[0].wait()
 
     def near_first(n):
         return (z + jnp.where((n & 1) == 1, (n + 1) >> 1, LINE - (n >> 1))) & 7
@@ -215,7 +212,7 @@
 
     def to_line(n):
         zz = near_first(LINE - 1 - n)
-        send(x_ref, line_buf.at[z], line_send, line_recv.at[z], line(zz))
+        send(x_hbm, line_buf.at[z], line_send, line_recv.at[z], line(zz))
 
     def spread(start):
         def each(n):
@@ -243,9 +240,9 @@
             def each(n):
                 dev = (first_group(s) + n) * GROUP + residue
                 if start:
-                    send(x_ref, dst, relay_send, sem, dev)
+                    send(x_hbm, dst, relay_send, sem, dev)
                 else:
-                    sent(x_ref, relay_send, dev)
+                    sent(x_hbm, relay_send, dev)
 
             loop(groups_of(s), each)
 
@@ -253,6 +250,9 @@
 
     loop(LINE, to_line)
     owned(to_relays(True))
+
+    for load in loads:
+        load.start()
 
     here = []
     for yy in (2, 1, 3, 0):
@@ -261,7 +261,7 @@
         for k in [first_row + i for i in range(ROWS_AT[yy])]:
             here.append((k, jnp.where(k < SEGS, tri(k), 2 * DEVICES), low))
 
-    for load in loads[1:]:
+    for load in loads:
         load.wait()
 
     def split_tile(k):
@@ -340,7 +340,14 @@
             base + ((first_share(row) + p) & 7),
         )
 
-    def all_sent(which, n, sem):
+    def all_sent(which, s, same_y, sem):
+        n = shares(s)
+        for turn in range(2):
+            p = ((residue - first_share(s)) & 7) + GROUP * turn
+            mine = p < shares(s)
+            if same_y:
+                mine = jnp.logical_and(mine, ((first_share(s) + p) >> 6) == y)
+            n = n - mine.astype(jnp.int32)
         for count in range(WINDOW - 3, WINDOW + 1):
             @pl.when(n == count)
             def _():
@@ -349,13 +356,11 @@
     def place_of(owner, s):
         return jnp.where(seg_of(SHARE * owner) == s, 0, 1)
 
-    def slot_of(owner, s):
-        return place_of(owner, s) * (KEYS + SEGS)
-
     def col_parts(p):
         owner = first_share(col) + p
-        at = slot_of(owner, col) + KEYS + row
-        send(chunk(1, p), arrived.at[at], col_send, arrive_recv.at[at], owner)
+        at = rank_of(me) * 2 + (p >> 3)
+        dev = (((owner >> 6) << 3) + z) * GROUP + (owner & 7)
+        send(chunk(1, p), col_buf.at[at], col_send, col_recv.at[at], dev)
 
     @pl.when(works)
     def _():
@@ -401,29 +406,42 @@
                 part_sum[key, turn] = lax.fori_loop(
                     0, count, each, jnp.zeros((ROWS, WIDTH), jnp.float32)
                 )
-                at = slot_of(owner, s) + group - first_group(s)
+                at = place_of(owner, s) * KEYS + group - first_group(s)
                 send(src, arrived.at[at], sum_send, arrive_recv.at[at], owner)
             else:
                 sent(src, sum_send, owner)
 
         return body
 
+    def add_cols(n):
+        zz = near_first(LINE - 1 - n)
+        col_sum[zz] = jnp.zeros((ROWS, WIDTH), jnp.float32)
+
+        def body(dev, s, p):
+            at = rank_of(dev) * 2 + (p >> 3)
+            landed(col_buf.at[at], col_recv.at[at])
+            col_sum[zz] = col_sum[zz] + col_buf[at]
+
+        targets(zz, body)
+        at = 2 * KEYS + z
+        send(col_sum.at[zz], arrived.at[at], back_send, arrive_recv.at[at], line(zz))
+
     relayed(add_parts(True))
+    loop(LINE, add_cols)
 
     def each(at, total):
         landed(arrived.at[at], arrive_recv.at[at])
         return total + arrived[at]
 
     def collect(w, s, total):
-        start = w * (KEYS + SEGS)
-        total = lax.fori_loop(start + KEYS + s, start + KEYS + SEGS, each, total)
-        return lax.fori_loop(start, start + groups_of(s), each, total)
+        return lax.fori_loop(w * KEYS, w * KEYS + groups_of(s), each, total)
 
     def put(total):
         for t in range(SHARE):
             image_ref[t] = total[t * VEC:(t + 1) * VEC]
 
-    put(collect(0, seg_a, jnp.zeros((ROWS, WIDTH), jnp.float32)))
+    total = collect(0, seg_a, jnp.zeros((ROWS, WIDTH), jnp.float32))
+    put(lax.fori_loop(2 * KEYS, 2 * KEYS + LINE, each, total))
 
     @pl.when(two)
     def _():
@@ -437,17 +455,16 @@
         jnp.concatenate([flat(x_ref), image], axis=0), image, NT_DIMS,
         precision=lax.Precision.HIGHEST, preferred_element_type=jnp.float32,
     )
-    gram_own[0] = jnp.zeros((VEC, WIDTH), jnp.float32)
-    gram_own[0, :, 0:VEC] = both[:VEC]
-    gram_own[0, :, VEC:2 * VEC] = both[VEC:]
-
-    def hops(m):
-        return [0, 1, 2, 1][m >> 3] + [0, 1, 2, 1][(m >> 1) & 3]
+    gram_tile[...] = jnp.zeros((VEC, WIDTH), jnp.float32)
+    gram_tile[:, 0:VEC] = both[:VEC]
+    gram_tile[:, VEC:2 * VEC] = both[VEC:]
+    moved = pltpu.roll(gram_tile[...], 0, 1, stride=2 * VEC, stride_axis=0)
+    gram_own[0] = jnp.sum(moved, axis=0, keepdims=True)
 
     rank = rank_of(me)
     circles = (
         (gram_a, z, LINE, [line((z + dz) & 7) for dz in (4, 3, 5, 2, 6, 1, 7)]),
-        (gram_b, rank, PLANE, [plane(rank ^ m) for m in sorted(range(1, PLANE), key=hops, reverse=True)]),
+        (gram_b, rank, PLANE, [plane(rank ^ m) for m in far_first]),
     )
     for n, (buf, rank, size, partners) in enumerate(circles):
         for dev in partners:
@@ -462,15 +479,13 @@
 
             @pl.when(off_diagonal)
             def _():
-                p = (residue - first_share(row)) & 7
-                n_sent = shares(row) - 1 - (p + GROUP < shares(row)).astype(jnp.int32)
-                all_sent(0, n_sent, part_send)
+                all_sent(0, row, False, part_send)
 
             @pl.when(works)
             def _():
-                p = me - first_share(col)
-                mine = jnp.logical_and(p >= 0, p < shares(col)).astype(jnp.int32)
-                all_sent(1, shares(col) - mine, col_send)
+                all_sent(1, col, True, col_send)
+
+            landed(col_sum.at[pl.ds(0, LINE - 1)], back_send)
 
         landed(buf.at[pl.ds(0, size - 1)], gram_recv.at[n])
         terms = [buf[q] for q in range(size)]
@@ -493,7 +508,7 @@
         kernel,
         out_shape=(
             pltpu.VMEM((SHARE, VEC, WIDTH), f32),
-            pltpu.VMEM((VEC, WIDTH), f32),
+            pltpu.VMEM((1, WIDTH), f32),
         ),
         in_specs=[pl.BlockSpec(memory_space=pl.ANY)] * 7,
         out_specs=(vmem, vmem),
@@ -511,15 +526,18 @@
             pltpu.VMEM((WINDOW * SHARE, VEC, WIDTH), f32),
             pltpu.VMEM((KEYS, 2, SHARE, VEC, WIDTH), f32),
             pltpu.VMEM((LINE, SHARE, VEC, WIDTH), f32),
+            pltpu.VMEM((2 * PLANE, ROWS, WIDTH), f32),
+            pltpu.VMEM((LINE, ROWS, WIDTH), f32),
             pltpu.VMEM((SLOTS * VEC, WIDTH), f32),
             pltpu.VMEM((SLOTS * VEC, WIDTH), f32),
             pltpu.VMEM((2, PAD * VEC, WIDTH), f32),
             pltpu.VMEM((2, GROUP, ROWS, WIDTH), f32),
             pltpu.VMEM((KEYS, 2, ROWS, WIDTH), f32),
-            pltpu.VMEM((2 * (KEYS + SEGS), ROWS, WIDTH), f32),
-            pltpu.VMEM((2, VEC, WIDTH), f32),
-            pltpu.VMEM((LINE, VEC, WIDTH), f32),
-            pltpu.VMEM((PLANE, VEC, WIDTH), f32),
+            pltpu.VMEM((2 * KEYS + LINE, ROWS, WIDTH), f32),
+            pltpu.VMEM((VEC, WIDTH), f32),
+            pltpu.VMEM((2, 1, WIDTH), f32),
+            pltpu.VMEM((LINE, 1, WIDTH), f32),
+            pltpu.VMEM((PLANE, 1, WIDTH), f32),
             dma((7,)),
             dma,
             dma((KEYS, 2)),
@@ -532,7 +550,9 @@
             dma((2, GROUP)),
             dma,
             dma,
-            dma((2 * (KEYS + SEGS),)),
+            dma((2 * PLANE,)),
+            dma,
+            dma((2 * KEYS + LINE,)),
             dma((2,)),
             dma((2,)),
         ],
@@ -543,7 +563,8 @@
         tiles, tile_rows, tile_cols, tile_rows.reshape(1, SLOTS), tile_cols.reshape(1, SLOTS),
         counts, block_vectors,
     )
-    return image, grams[:, :VEC], grams[:, VEC:2 * VEC]
+    grams = grams.reshape(VEC, 2 * VEC)
+    return image, grams[:, :VEC], grams[:, VEC:]
 
 
 def solution(mesh):

time: 50.9 us -> 50.3 us (0.988)
  Pallas kernels: 48.2 us -> 46.4 us
  other arithmetic: 0 us -> 0.66 us
  local copies, waits for them, and re-layouts: 1.27 us -> 1.87 us
    pallas_call x1, Pallas kernels: 48.2 us -> 46.4 us  [per_device(): pl.pallas_call(kernel, out_shape=(pltpu.VMEM((SHARE, VEC, WIDTH), f32), p...]
    pallas_call x0 -> x1, other arithmetic: none -> 0.66 us  [per_device(): pl.pallas_call(kernel, out_shape=(pltpu.VMEM((SHARE, VEC, WIDTH), f32), p...]
    pallas_call x0 -> x1, local copies, waits for them, and re-layouts: none -> 0.51 us  [per_device(): pl.pallas_call(kernel, out_shape=(pltpu.VMEM((SHARE, VEC, WIDTH), f32), p...]
where the time goes in v8:
time: 50.3 us; the launch traced here: 50.2 us
  Pallas kernels  46.4 us (92%)
  local copies, waits for them, and re-layouts  1.87 us (4%)
  between operations  1.29 us (3%)
  other arithmetic  0.66 us (1%)
    pallas_call x1, Pallas kernels, per_device(): pl.pallas_call(kernel, out_shape=(pltpu.VMEM((SHARE, VEC, WIDTH), f32), p...  46.4 us

profile of v8, /device:TPU:1, one launch (start us, length us, event | category | flops | bytes accessed | tf_op | source)
XLA Modules:
  0.0 50.2 jit_solution(4809816549535057758)
XLA Ops:
  1.3 46.4 %shard_map.76 = (f32[4,8,128]{2,1,0:T(8,128)S(1)}, f32[1,128]{1,0:T(1,128)S(1)}) custom-call(f32[32,128,128]{2,1,0:T(8,128)} %tiles_ref.1, s32[32]{0:T(128)} %rows_hbm.1, s32[32]{0:T(128)} %cols_hbm.1, s32[1,32]{1,0:T(1,128)} %bitcast.2, s32[1,32]{1,0:T(1,128)} %bitcast.3, s32[1]{0:T(128)S(6)} %copy.10.count_hbm, f32[4,8,128]{2,1,0:T(8,128)} %x_hbm.1), custom_call_target="tpu_custom_call" | custom-call | tf_op jit(solution)/shard_map/pallas_call | solution.py:507
  47.6 0.6 %copy.9 = f32[4,8,128]{2,1,0:T(8,128)} copy(f32[4,8,128]{2,1,0:T(8,128)S(1)} %get-tuple-element.9) | data formatting | bytes 32768
  48.2 0.5 %broadcast.3 = f32[]{:T(128)} broadcast(f32[]{:T(128)} %constant.8), dimensions={} | broadcast | bytes 8 | tf_op jit(solution)/shard_map/pallas_call | solution.py:507
  48.8 0.7 %reduce.3 = f32[128]{0:T(128)S(1)} reduce(f32[1,128]{1,0:T(1,128)S(1)} %get-tuple-element.6, f32[]{:T(128)} %broadcast.3), dimensions={0}, to_apply=%get-tuple-element.6.reduce_sub_computation.3 | reduce | bytes 1028 | tf_op jit(solution)/shard_map/pallas_call | solution.py:507
  49.4 0.1 reshape.17
  49.5 0.7 %fusion = (f32[8,8]{1,0:T(8,128)}, f32[8,8]{1,0:T(8,128)}) fusion(f32[8,16]{1,0:T(8,128)S(1)} %reshape.17), kind=kLoop, calls=%fused_computation | loop fusion | bytes 1024 | tf_op jit(solution)/shard_map/slice | solution.py:567

commit v9 on v8

--- a/solution.py
+++ b/solution.py
@@ -494,7 +494,12 @@
         if n == 0:
             gram_own[1] = terms[0]
         else:
-            grams_ref[...] = terms[0] * (1.0 / (TILES * WIDTH))
+            out = jnp.broadcast_to(terms[0] * (1.0 / (TILES * WIDTH)), (VEC, WIDTH))
+            block = lax.broadcasted_iota(jnp.int32, (VEC, WIDTH), 1) >> 4
+            out = jnp.where(block == lax.broadcasted_iota(jnp.int32, (VEC, WIDTH), 0), out, 0.0)
+            for shift in (64, 32, 16):
+                out = out + pltpu.roll(out, shift, 1)
+            grams_ref[...] = out
 
     for n, (buf, _rank, size, _partners) in enumerate(circles):
         landed(buf.at[pl.ds(0, size - 1)], gram_send.at[n])
@@ -508,7 +513,7 @@
         kernel,
         out_shape=(
             pltpu.VMEM((SHARE, VEC, WIDTH), f32),
-            pltpu.VMEM((1, WIDTH), f32),
+            pltpu.VMEM((VEC, WIDTH), f32),
         ),
         in_specs=[pl.BlockSpec(memory_space=pl.ANY)] * 7,
         out_specs=(vmem, vmem),
@@ -563,8 +568,7 @@
         tiles, tile_rows, tile_cols, tile_rows.reshape(1, SLOTS), tile_cols.reshape(1, SLOTS),
         counts, block_vectors,
     )
-    grams = grams.reshape(VEC, 2 * VEC)
-    return image, grams[:, :VEC], grams[:, VEC:]
+    return image, grams[:, :VEC], grams[:, VEC:2 * VEC]
 
 
 def solution(mesh):

time: 50.3 us -> 49.2 us (0.978)
  other arithmetic: 0.66 us -> 0 us
  local copies, waits for them, and re-layouts: 1.87 us -> 1.27 us
    pallas_call x1 -> x0, other arithmetic: 0.66 us -> none  [per_device(): pl.pallas_call(kernel, out_shape=(pltpu.VMEM((SHARE, VEC, WIDTH), f32), p...]
    pallas_call x1 -> x0, local copies, waits for them, and re-layouts: 0.51 us -> none  [per_device(): pl.pallas_call(kernel, out_shape=(pltpu.VMEM((SHARE, VEC, WIDTH), f32), p...]
where the time goes in v9:
time: 49.2 us; the launch traced here: 49.1 us
  Pallas kernels  46.6 us (95%)
  between operations  1.29 us (3%)
  local copies, waits for them, and re-layouts  1.27 us (3%)
    pallas_call x1, Pallas kernels, per_device(): pl.pallas_call(kernel, out_shape=(pltpu.VMEM((SHARE, VEC, WIDTH), f32), p...  46.6 us

profile of v9, /device:TPU:1, one launch (start us, length us, event | category | flops | bytes accessed | tf_op | source)
XLA Modules:
  0.0 49.1 jit_solution(9596935258296351079)
XLA Ops:
  1.3 46.6 %shard_map.76 = (f32[4,8,128]{2,1,0:T(8,128)S(1)}, f32[8,128]{1,0:T(8,128)S(1)}) custom-call(f32[32,128,128]{2,1,0:T(8,128)} %tiles_ref.1, s32[32]{0:T(128)} %rows_hbm.1, s32[32]{0:T(128)} %cols_hbm.1, s32[1,32]{1,0:T(1,128)} %bitcast.2, s32[1,32]{1,0:T(1,128)} %bitcast.3, s32[1]{0:T(128)S(6)} %copy.10.count_hbm, f32[4,8,128]{2,1,0:T(8,128)} %x_hbm.1), custom_call_target="tpu_custom_call" | custom-call | tf_op jit(solution)/shard_map/pallas_call | solution.py:512
  47.8 0.6 %copy.9 = f32[4,8,128]{2,1,0:T(8,128)} copy(f32[4,8,128]{2,1,0:T(8,128)S(1)} %get-tuple-element.9) | data formatting | bytes 32768
  48.5 0.7 %fusion = (f32[8,8]{1,0:T(8,128)}, f32[8,8]{1,0:T(8,128)}) fusion(f32[8,128]{1,0:T(8,128)S(1)} %get-tuple-element.6), kind=kLoop, calls=%fused_computation | loop fusion | bytes 1024 | tf_op jit(solution)/shard_map/slice | solution.py:571

commit v10 on v9

--- a/solution.py
+++ b/solution.py
@@ -156,6 +156,16 @@
     def landed(dst, recv_sem):
         pltpu.make_async_copy(dst, dst, recv_sem).wait()
 
+    def all_landed(held, n, limit, recv_sem):
+        def narrow(low, high):
+            if high - low > 1:
+                mid = (low + high) // 2
+                lax.cond(n < mid, lambda: narrow(low, mid), lambda: narrow(mid, high))
+            elif low:
+                landed(held.at[pl.ds(0, low)], recv_sem)
+
+        narrow(0, limit + 1)
+
     barrier = pltpu.get_barrier_semaphore()
 
     def greet(dev):
@@ -194,21 +204,36 @@
     def near_first(n):
         return (z + jnp.where((n & 1) == 1, (n + 1) >> 1, LINE - (n >> 1))) & 7
 
+    def at_my_z(s, k, first, low):
+        return jnp.logical_and(((first + s - low) >> 3) == 0, s <= k)
+
+    def owned_by(zz):
+        owner = line(zz)
+        a = seg_of(SHARE * owner)
+        return owner, a, seg_of(SHARE * owner + SHARE - 1) - a + 1
+
     def targets(zz, body):
-        owner = line(zz)
-        a, b = seg_of(SHARE * owner), seg_of(SHARE * owner + SHARE - 1)
+        owner, a, count = owned_by(zz)
 
         def one(w):
             s = a + w
             p = owner - first_share(s)
             for k, first, low in here:
-                dev = first + s
-
-                @pl.when(jnp.logical_and(((dev - low) >> 3) == 0, s <= k))
-                def _(dev=dev):
-                    body(dev, s, p)
-
-        loop(1 + (b > a).astype(jnp.int32), one)
+                @pl.when(at_my_z(s, k, first, low))
+                def _(first=first):
+                    body(first + s, s, p)
+
+        loop(count, one)
+
+    def count_targets(zz, total):
+        _owner, a, count = owned_by(zz)
+
+        def one(w, total):
+            for k, first, low in here:
+                total = total + at_my_z(a + w, k, first, low).astype(jnp.int32)
+            return total
+
+        return lax.fori_loop(0, count, one, total)
 
     def to_line(n):
         zz = near_first(LINE - 1 - n)
@@ -336,7 +361,7 @@
     def row_parts(p):
         turn = p >> 3
         send(
-            chunk(0, p), part_buf.at[turn, residue], part_send, part_recv.at[turn, residue],
+            chunk(0, p), part_buf.at[turn * GROUP + residue], part_send, part_recv,
             base + ((first_share(row) + p) & 7),
         )
 
@@ -360,7 +385,7 @@
         owner = first_share(col) + p
         at = rank_of(me) * 2 + (p >> 3)
         dev = (((owner >> 6) << 3) + z) * GROUP + (owner & 7)
-        send(chunk(1, p), col_buf.at[at], col_send, col_recv.at[at], dev)
+        send(chunk(1, p), col_buf.at[at], col_send, col_recv, dev)
 
     @pl.when(works)
     def _():
@@ -400,14 +425,13 @@
 
                 def each(i, total):
                     rank = (low + i) & 7
-                    landed(part_buf.at[turn, rank], part_recv.at[turn, rank])
-                    return total + part_buf[turn, rank]
+                    return total + part_buf[turn * GROUP + rank]
 
                 part_sum[key, turn] = lax.fori_loop(
                     0, count, each, jnp.zeros((ROWS, WIDTH), jnp.float32)
                 )
                 at = place_of(owner, s) * KEYS + group - first_group(s)
-                send(src, arrived.at[at], sum_send, arrive_recv.at[at], owner)
+                send(src, arrived.at[at], sum_send, arrive_recv, owner)
             else:
                 sent(src, sum_send, owner)
 
@@ -419,22 +443,33 @@
 
         def body(dev, s, p):
             at = rank_of(dev) * 2 + (p >> 3)
-            landed(col_buf.at[at], col_recv.at[at])
             col_sum[zz] = col_sum[zz] + col_buf[at]
 
         targets(zz, body)
         at = 2 * KEYS + z
-        send(col_sum.at[zz], arrived.at[at], back_send, arrive_recv.at[at], line(zz))
-
+        send(col_sum.at[zz], arrived.at[at], back_send, arrive_recv, line(zz))
+
+    def parts_of(n, total):
+        s = top + n
+        start = (residue - first_share(s)) & 7
+        turns = (start < shares(s)).astype(jnp.int32) + (start + GROUP < shares(s)).astype(jnp.int32)
+        return total + turns * jnp.maximum(span(s)[1], 0)
+
+    n_parts = lax.fori_loop(0, rows_here, parts_of, 0)
+    n_cols = lax.fori_loop(0, LINE, count_targets, 0)
+    all_landed(part_buf, n_parts, 2 * GROUP, part_recv)
     relayed(add_parts(True))
+    all_landed(col_buf, n_cols, 2 * PLANE, col_recv)
     loop(LINE, add_cols)
 
     def each(at, total):
-        landed(arrived.at[at], arrive_recv.at[at])
         return total + arrived[at]
 
     def collect(w, s, total):
         return lax.fori_loop(w * KEYS, w * KEYS + groups_of(s), each, total)
+
+    n_arrived = LINE + groups_of(seg_a) + jnp.where(two, groups_of(seg_b), 0)
+    all_landed(arrived, n_arrived, 2 * KEYS + LINE, arrive_recv)
 
     def put(total):
         for t in range(SHARE):
@@ -536,7 +571,7 @@
             pltpu.VMEM((SLOTS * VEC, WIDTH), f32),
             pltpu.VMEM((SLOTS * VEC, WIDTH), f32),
             pltpu.VMEM((2, PAD * VEC, WIDTH), f32),
-            pltpu.VMEM((2, GROUP, ROWS, WIDTH), f32),
+            pltpu.VMEM((2 * GROUP, ROWS, WIDTH), f32),
             pltpu.VMEM((KEYS, 2, ROWS, WIDTH), f32),
             pltpu.VMEM((2 * KEYS + LINE, ROWS, WIDTH), f32),
             pltpu.VMEM((VEC, WIDTH), f32),
@@ -552,12 +587,12 @@
             dma,
             dma((2,)),
             dma,
-            dma((2, GROUP)),
-            dma,
-            dma,
-            dma((2 * PLANE,)),
-            dma,
-            dma((2 * KEYS + LINE,)),
+            dma,
+            dma,
+            dma,
+            dma,
+            dma,
+            dma,
             dma((2,)),
             dma((2,)),
         ],

time: 49.2 us -> 49.1 us (level)
  no operation moved by 1% of the time
where the time goes in v10:
time: 49.1 us; the launch traced here: 49 us
  Pallas kernels  46.4 us (95%)
  between operations  1.29 us (3%)
  local copies, waits for them, and re-layouts  1.27 us (3%)
    pallas_call x1, Pallas kernels, per_device(): pl.pallas_call(kernel, out_shape=(pltpu.VMEM((SHARE, VEC, WIDTH), f32), p...  46.4 us

profile of v10, /device:TPU:1, one launch (start us, length us, event | category | flops | bytes accessed | tf_op | source)
XLA Modules:
  0.0 49.0 jit_solution(14792503585382309702)
XLA Ops:
  1.3 46.4 %shard_map.76 = (f32[4,8,128]{2,1,0:T(8,128)S(1)}, f32[8,128]{1,0:T(8,128)S(1)}) custom-call(f32[32,128,128]{2,1,0:T(8,128)} %tiles_ref.1, s32[32]{0:T(128)} %rows_hbm.1, s32[32]{0:T(128)} %cols_hbm.1, s32[1,32]{1,0:T(1,128)} %bitcast.2, s32[1,32]{1,0:T(1,128)} %bitcast.3, s32[1]{0:T(128)S(6)} %copy.10.count_hbm, f32[4,8,128]{2,1,0:T(8,128)} %x_hbm.1), custom_call_target="tpu_custom_call" | custom-call | tf_op jit(solution)/shard_map/pallas_call | solution.py:547
  47.7 0.6 %copy.9 = f32[4,8,128]{2,1,0:T(8,128)} copy(f32[4,8,128]{2,1,0:T(8,128)S(1)} %get-tuple-element.9) | data formatting | bytes 32768
  48.3 0.7 %fusion = (f32[8,8]{1,0:T(8,128)}, f32[8,8]{1,0:T(8,128)}) fusion(f32[8,128]{1,0:T(8,128)S(1)} %get-tuple-element.6), kind=kLoop, calls=%fused_computation | loop fusion | bytes 1024 | tf_op jit(solution)/shard_map/slice | solution.py:606

commit v11 on v10

--- a/solution.py
+++ b/solution.py
@@ -236,7 +236,7 @@
         return lax.fori_loop(0, count, one, total)
 
     def to_line(n):
-        zz = near_first(LINE - 1 - n)
+        zz = near_first(n)
         send(x_hbm, line_buf.at[z], line_send, line_recv.at[z], line(zz))
 
     def spread(start):

time: 49.1 us -> 48.8 us (level)
  no operation moved by 1% of the time
where the time goes in v11:
time: 48.8 us; the launch traced here: 48.6 us
  Pallas kernels  46.1 us (94%)
  between operations  1.29 us (3%)
  local copies, waits for them, and re-layouts  1.27 us (3%)
    pallas_call x1, Pallas kernels, per_device(): pl.pallas_call(kernel, out_shape=(pltpu.VMEM((SHARE, VEC, WIDTH), f32), p...  46.1 us

profile of v11, /device:TPU:1, one launch (start us, length us, event | category | flops | bytes accessed | tf_op | source)
XLA Modules:
  0.0 48.6 jit_solution(10938499624284595586)
XLA Ops:
  1.3 46.1 %shard_map.76 = (f32[4,8,128]{2,1,0:T(8,128)S(1)}, f32[8,128]{1,0:T(8,128)S(1)}) custom-call(f32[32,128,128]{2,1,0:T(8,128)} %tiles_ref.1, s32[32]{0:T(128)} %rows_hbm.1, s32[32]{0:T(128)} %cols_hbm.1, s32[1,32]{1,0:T(1,128)} %bitcast.2, s32[1,32]{1,0:T(1,128)} %bitcast.3, s32[1]{0:T(128)S(6)} %copy.10.count_hbm, f32[4,8,128]{2,1,0:T(8,128)} %x_hbm.1), custom_call_target="tpu_custom_call" | custom-call | tf_op jit(solution)/shard_map/pallas_call | solution.py:547
  47.4 0.6 %copy.9 = f32[4,8,128]{2,1,0:T(8,128)} copy(f32[4,8,128]{2,1,0:T(8,128)S(1)} %get-tuple-element.9) | data formatting | bytes 32768
  48.0 0.7 %fusion = (f32[8,8]{1,0:T(8,128)}, f32[8,8]{1,0:T(8,128)}) fusion(f32[8,128]{1,0:T(8,128)S(1)} %get-tuple-element.6), kind=kLoop, calls=%fused_computation | loop fusion | bytes 1024 | tf_op jit(solution)/shard_map/slice | solution.py:606

commit v12 on v11

--- a/solution.py
+++ b/solution.py
@@ -486,10 +486,12 @@
         return jnp.concatenate([ref[t] for t in range(SHARE)], axis=1)
 
     image = flat(image_ref)
+    left = jnp.concatenate(split(jnp.concatenate([flat(x_ref), image], axis=0)), axis=0)
     both = lax.dot_general(
-        jnp.concatenate([flat(x_ref), image], axis=0), image, NT_DIMS,
-        precision=lax.Precision.HIGHEST, preferred_element_type=jnp.float32,
+        jnp.concatenate([left, left], axis=1), jnp.concatenate(split(image), axis=1), NT_DIMS,
+        preferred_element_type=jnp.float32,
     )
+    both = both[:2 * VEC] + both[2 * VEC:]
     gram_tile[...] = jnp.zeros((VEC, WIDTH), jnp.float32)
     gram_tile[:, 0:VEC] = both[:VEC]
     gram_tile[:, VEC:2 * VEC] = both[VEC:]

time: 48.8 us -> 48.7 us (level)
  no operation moved by 1% of the time
where the time goes in v12:
time: 48.7 us; the launch traced here: 48.6 us
  Pallas kernels  46.1 us (95%)
  between operations  1.29 us (3%)
  local copies, waits for them, and re-layouts  1.27 us (3%)
    pallas_call x1, Pallas kernels, per_device(): pl.pallas_call(kernel, out_shape=(pltpu.VMEM((SHARE, VEC, WIDTH), f32), p...  46.1 us

profile of v12, /device:TPU:1, one launch (start us, length us, event | category | flops | bytes accessed | tf_op | source)
XLA Modules:
  0.0 48.6 jit_solution(6238447502422361130)
XLA Ops:
  1.3 46.1 %shard_map.76 = (f32[4,8,128]{2,1,0:T(8,128)S(1)}, f32[8,128]{1,0:T(8,128)S(1)}) custom-call(f32[32,128,128]{2,1,0:T(8,128)} %tiles_ref.1, s32[32]{0:T(128)} %rows_hbm.1, s32[32]{0:T(128)} %cols_hbm.1, s32[1,32]{1,0:T(1,128)} %bitcast.2, s32[1,32]{1,0:T(1,128)} %bitcast.3, s32[1]{0:T(128)S(6)} %copy.10.count_hbm, f32[4,8,128]{2,1,0:T(8,128)} %x_hbm.1), custom_call_target="tpu_custom_call" | custom-call | tf_op jit(solution)/shard_map/pallas_call | solution.py:549
  47.3 0.6 %copy.9 = f32[4,8,128]{2,1,0:T(8,128)} copy(f32[4,8,128]{2,1,0:T(8,128)S(1)} %get-tuple-element.9) | data formatting | bytes 32768
  48.0 0.7 %fusion = (f32[8,8]{1,0:T(8,128)}, f32[8,8]{1,0:T(8,128)}) fusion(f32[8,128]{1,0:T(8,128)S(1)} %get-tuple-element.6), kind=kLoop, calls=%fused_computation | loop fusion | bytes 1024 | tf_op jit(solution)/shard_map/slice | solution.py:608

commit v13 on v11

--- a/solution.py
+++ b/solution.py
@@ -411,10 +411,6 @@
 
         loop(shares(col), col_parts)
 
-    landed(line_buf.at[pl.ds(0, LINE - 1)], line_send)
-    owned(to_relays(False))
-    spread(False)
-    relayed(pass_on(False))
 
     def add_parts(start):
         def body(s, p, key, turn):
@@ -510,6 +506,10 @@
 
         buf[rank] = gram_own[n]
         if n == 0:
+            landed(line_buf.at[pl.ds(0, LINE - 1)], line_send)
+            owned(to_relays(False))
+            spread(False)
+            relayed(pass_on(False))
             relayed(add_parts(False))
 
             @pl.when(off_diagonal)

time: 48.8 us -> 48.8 us (level)
  no operation moved by 1% of the time
where the time goes in v13:
time: 48.8 us; the launch traced here: 48.6 us
  Pallas kernels  46.1 us (94%)
  between operations  1.29 us (3%)
  local copies, waits for them, and re-layouts  1.27 us (3%)
    pallas_call x1, Pallas kernels, per_device(): pl.pallas_call(kernel, out_shape=(pltpu.VMEM((SHARE, VEC, WIDTH), f32), p...  46.1 us

profile of v13, /device:TPU:1, one launch (start us, length us, event | category | flops | bytes accessed | tf_op | source)
XLA Modules:
  0.0 48.6 jit_solution(309277466451551193)
XLA Ops:
  1.3 46.1 %shard_map.76 = (f32[4,8,128]{2,1,0:T(8,128)S(1)}, f32[8,128]{1,0:T(8,128)S(1)}) custom-call(f32[32,128,128]{2,1,0:T(8,128)} %tiles_ref.1, s32[32]{0:T(128)} %rows_hbm.1, s32[32]{0:T(128)} %cols_hbm.1, s32[1,32]{1,0:T(1,128)} %bitcast.2, s32[1,32]{1,0:T(1,128)} %bitcast.3, s32[1]{0:T(128)S(6)} %copy.10.count_hbm, f32[4,8,128]{2,1,0:T(8,128)} %x_hbm.1), custom_call_target="tpu_custom_call" | custom-call | tf_op jit(solution)/shard_map/pallas_call | solution.py:547
  47.4 0.6 %copy.9 = f32[4,8,128]{2,1,0:T(8,128)} copy(f32[4,8,128]{2,1,0:T(8,128)S(1)} %get-tuple-element.9) | data formatting | bytes 32768
  48.0 0.7 %fusion = (f32[8,8]{1,0:T(8,128)}, f32[8,8]{1,0:T(8,128)}) fusion(f32[8,128]{1,0:T(8,128)S(1)} %get-tuple-element.6), kind=kLoop, calls=%fused_computation | loop fusion | bytes 1024 | tf_op jit(solution)/shard_map/slice | solution.py:606
